TPU v7x, 256 devices: a whole 4x4x8 slice. The times are simulated.
256 devices in a mesh: ctx: 64 (over x, z, core), rep: 4 (over y).
Axes of the slice: x: 4, y: 4, z: 8, core: 2. Of those that a mesh axis runs over, the one named last changes fastest.
Arguments:
- queries: bfloat16 [8, 2, 128, 192], P('rep', None, 'ctx'), parts along dimension 0, may hold values from -6 to 6
- key_absorb: bfloat16 [128, 128, 512], P('ctx'), may hold values from -0.5 to 0.5
- latent_cache: bfloat16 [8, 262144, 576], P('rep', 'ctx'), parts along dimension 0, may hold values from -600 to 600
- page_order: int32 [8, 2048], P('rep', 'ctx'), parts along dimension 0, may hold values from 0 to 2047, each once within a row
- lengths: int32 [8], P('rep'), parts along dimension 0, may hold values from 65536 to 262144
- kerple_scale: float32 [128], replicated, may hold values from 0.05 to 2
- kerple_rate: float32 [128], replicated, may hold values from 0.005 to 0.5
- value_up: bfloat16 [128, 512, 128], P('ctx'), may hold values from -0.25 to 0.25
- output_weight: bfloat16 [16384, 7168], P('ctx'), may hold values from -0.125 to 0.125
Outputs:
- attn_out: bfloat16 [8, 2, 7168], P('rep', None, 'ctx'), parts along dimension 0
There are 4 independent parts, one for each index of `rep`. A program takes and returns all parts, laid end to end along the dimension named above; an argument that names none is the same for every part. Nothing has to cross between parts.
All inputs are finite; a program needn't handle non-finite values.
Results may differ from a plain program's by a relative error of at most 0.015.
Values may be sent and summed in bfloat16 or wider, within the bound.
A program may use at most 192 MiB of HBM per device.

v0:
```python
import jax
import jax.numpy as jnp
from jax import lax
from jax.sharding import PartitionSpec as P

NOPE = 128
ROPE = 64
LAT = 512
PAGE = 128


masked_score = -1e30


def block_terms(full_query, cache_block, key_pos, query_pos, kerple_scale, kerple_rate):
    distance = query_pos[:, :, None] - key_pos[:, None, :]
    visible = (distance >= 0)[:, :, None, :]
    spread = jnp.maximum(distance, 0).astype(jnp.float32)[:, :, None, :]
    log_bias = kerple_scale[:, None] * jnp.log1p(kerple_rate[:, None] * spread)
    softmax_scale = (NOPE + ROPE) ** (-0.5)
    scores = jnp.einsum(
        "bqhc,btc->bqht", full_query, cache_block, preferred_element_type=jnp.float32
    )
    scores = jnp.where(visible, scores * softmax_scale - log_bias, masked_score)
    row_max = jnp.max(scores, axis=-1)
    weights = jnp.where(visible, jnp.exp(scores - row_max[..., None]), 0.0)
    row_total = jnp.sum(weights, axis=-1)
    summed = jnp.einsum(
        "bqht,btc->bqhc",
        weights.astype(jnp.bfloat16),
        cache_block[..., :LAT],
        preferred_element_type=jnp.float32,
    )
    return (row_max, row_total, summed)


def per_device(
    queries,
    key_absorb,
    latent_cache,
    page_order,
    lengths,
    kerple_scale,
    kerple_rate,
    value_up,
    output_weight,
):
    requests, query_len, local_heads, _ = queries.shape
    keys_dev = latent_cache.shape[1]
    latent_query = jnp.einsum(
        "bqhn,hnc->bqhc", queries[..., :NOPE], key_absorb, preferred_element_type=jnp.float32
    ).astype(jnp.bfloat16)
    own_query = jnp.concatenate([latent_query, queries[..., NOPE:]], axis=-1)
    full_query = lax.all_gather(own_query, "ctx", axis=2, tiled=True)
    offsets = jnp.arange(PAGE, dtype=jnp.int32)
    key_pos = (page_order[:, :, None] * PAGE + offsets[None, None, :]).reshape(requests, keys_dev)
    query_pos = lengths[:, None] - query_len + jnp.arange(query_len, dtype=jnp.int32)[None, :]
    partial_terms = block_terms(
        full_query, latent_cache, key_pos, query_pos, kerple_scale, kerple_rate
    )
    row_max, row_total, summed = partial_terms
    global_max = lax.pmax(row_max, "ctx")
    factor = jnp.exp(row_max - global_max)
    shared_total, shared_sum = (
        lax.psum_scatter(row_total * factor, "ctx", scatter_dimension=2, tiled=True),
        lax.psum_scatter(summed * factor[..., None], "ctx", scatter_dimension=2, tiled=True),
    )
    attn_latent = (shared_sum / shared_total[..., None]).astype(jnp.bfloat16)
    up_values = jnp.einsum(
        "bqhc,hcv->bqhv", attn_latent, value_up, preferred_element_type=jnp.float32
    ).astype(jnp.bfloat16)
    flat_values = up_values.reshape(requests * query_len, local_heads * up_values.shape[-1])
    partial_out = jnp.dot(flat_values, output_weight, preferred_element_type=jnp.float32).reshape(
        requests, query_len, output_weight.shape[1]
    )
    return lax.psum_scatter(partial_out, "ctx", scatter_dimension=2, tiled=True).astype(
        jnp.bfloat16
    )


def solution(mesh):
    in_specs = (
        P("rep", None, "ctx", None),
        P("ctx", None, None),
        P("rep", "ctx", None),
        P("rep", "ctx"),
        P("rep"),
        P(),
        P(),
        P("ctx", None, None),
        P("ctx", None),
    )
    out_specs = P("rep", None, "ctx")
    return jax.shard_map(
        per_device, mesh=mesh, in_specs=in_specs, out_specs=out_specs, check_vma=False
    )
```

profile of v0, /device:TPU:1, one launch (start us, length us, event | category | flops | bytes accessed | tf_op | source)
XLA Modules:
  0.0 560.8 jit_solution(4102203464076679294)
XLA Ops:
  6.5 0.0 copy-start
  6.5 0.0 all-reduce.4.cloned.1.call-start
  6.5 0.7 slice.9
  7.3 0.7 slice.10
  8.0 0.7 broadcast_add_fusion
  8.6 0.1 iota_add_fusion
  8.7 0.7 broadcast_multiply_fusion
  9.4 0.1 broadcast_bitcast_fusion
  9.5 0.1 subtract_compare_fusion
  9.6 0.1 fusion.25
  9.7 0.0 copy-done
  9.7 0.1 fusion.20
  9.9 54.8 %all_gather.3 = bf16[2,2,128,576]{3,1,0,2:T(2,128)(2,1)S(1)} all-gather(bf16[2,2,2,576]{3,1,0,2:T(2,128)(2,1)S(1)} %pad_maximum_fusion), channel_id=1, replica_groups=mesh['ctx'=64,'rep'=4] {'ctx'}, dimensions={2}, use_global_device_ids=true | all-gather | bytes 599040 | tf_op jit(solution)/shard_map/all_gather | solution.py:54
  64.8 13.1 %fusion.35 = (f32[2,2,128]{2,1,0:T(2,128)S(1)}, f32[2,2,128,4096]{3,2,1,0:T(8,128)}) fusion(f32[2,2,4096]{2,1,0:T(2,128)S(1)} %fusion.25, f32[128]{0:T(128)} %param.15, f32[128]{0:T(128)} %param.14, bf16[2,4096,576]{1,2,0:T(8,128)(2,1)} %param.11, bf16[2,2,128,576]{3,1,0,2:T(2,128)(2,1)S(1)} %all_gather.3, pred[2,2,4096]{2,1,0:T(4,128)(4,1)S(1)} %subtract_compare_fusion), kind=kOutput, calls=%fused_computation.43 | convolution fusion | flops 2428501504 | bytes 18500608 | tf_op jit(solution)/shard_map/bqhc,btc->bqht/dot_general | solution.py:21
  77.8 123.5 %pmax.7 = f32[2,2,128]{2,1,0:T(2,128)S(1)} all-reduce(f32[2,2,128]{2,1,0:T(2,128)S(1)} %get-tuple-element.7), channel_id=1, replica_groups=mesh['ctx'=64,'rep'=4] {'ctx'}, use_global_device_ids=true, to_apply=%region_1.2 | all-reduce | flops 512 | bytes 4096 | tf_op jit(solution)/shard_map/pmax | solution.py:62
  201.4 5.1 fusion.5
  206.5 0.0 copy-start.2
  206.5 0.0 copy-start.1
  206.5 8.2 %fusion.15 = f32[2,2,128,512]{3,2,1,0:T(8,128)S(1)} fusion(bf16[2,4096,576]{1,2,0:T(8,128)(2,1)} %param.11, f32[2,2,128,4096]{3,2,1,0:T(8,128)} %get-tuple-element.8, f32[2,2,128]{2,1,0:T(2,128)S(1)} %get-tuple-element.7, pred[2,2,4096]{2,1,0:T(4,128)(4,1)S(1)} %subtract_compare_fusion, f32[2,2,128]{2,1,0:T(2,128)S(1)} %get-tuple-element.6), kind=kOutput, calls=%fused_computation.14 | convolution fusion | flops 2154037248 | bytes 17846272 | tf_op jit(solution)/shard_map/bqht,btc->bqhc/dot_general | solution.py:28
  214.7 1.8 copy.19
  216.6 0.0 all-reduce.4.cloned.1.call-update
  216.6 0.0 reduce-scatter.5.cloned.1.call-start
  216.6 0.0 copy-done.2
  216.7 0.6 dynamic-slice
  217.9 126.7 %all-reduce.1 = f32[2,2,128]{2,1,0:T(2,128)S(1)} all-reduce(f32[2,2,128]{2,1,0:T(2,128)S(1)} %get-tuple-element.5), channel_id=3, replica_groups=mesh['ctx'=64,'rep'=4] {'ctx'}, use_global_device_ids=true, to_apply=%region_4.5.clone | all-reduce | flops 512 | bytes 4096
  344.6 0.1 constant_dynamic-slice_fusion
  344.7 0.1 copy.20
  344.8 52.1 %all-reduce.4.cloned.1.call-done = f32[2,2,128,512]{3,1,0,2:T(2,128)} async-done(((f32[2,2,128,512]{3,1,0,2:T(2,128)}), f32[2,2,128,512]{3,1,0,2:T(2,128)}) %all-reduce.4.cloned.1.call-update) | async-done | bytes 1048592
  396.9 0.0 copy-done.1
  396.9 0.9 fusion.21
  397.8 2.6 fusion.13
  400.5 6.8 %copy.28 = f32[2,2,7168]{1,0,2:T(2,128)} copy(f32[2,2,7168]{2,1,0:T(2,128)S(1)} %fusion.13) | data formatting | bytes 229376
  407.3 7.9 %reshape.58 = f32[7168,4]{1,0:T(8,128)} reshape(f32[7168,2,2]{2,1,0:T(2,128)} %bitcast.49) | data formatting | bytes 229376
  415.2 0.0 reduce-scatter.5.cloned.1.call-update
  415.2 137.1 %reduce-scatter.5.cloned.1.call-done = f32[112,4]{1,0:T(8,128)} async-done(((f32[7168,4]{1,0:T(8,128)}), f32[112,4]{1,0:T(8,128)}) %reduce-scatter.5.cloned.1.call-update) | async-done | bytes 1808
  552.4 0.9 reshape.59
  553.3 0.7 copy.29
  (5 shorter events, 0.1 us)
Async XLA Ops:
  6.5 3.2 copy-start
  6.5 390.4 %all-reduce.4.cloned.1.call-start = ((), (), s32[]{:S(2)}) async-start(), calls=%async_computation.2 | async-start | bytes 2097152
  206.5 10.2 %copy-start.2 = (u32[256]{0:T(256)S(1)}, u32[256]{0:T(256)}, u32[]{:S(2)}) copy-start(u32[256]{0:T(256)} %constant.23) | copy-start | bytes 3076
  206.5 190.4 %copy-start.1 = (bf16[2,512,128]{2,1,0:T(8,128)(2,1)S(1)}, bf16[2,512,128]{2,1,0:T(8,128)(2,1)}, u32[]{:S(2)}) copy-start(bf16[2,512,128]{2,1,0:T(8,128)(2,1)} %param.16) | copy-start | bytes 786436
  216.6 335.8 %reduce-scatter.5.cloned.1.call-start = ((), (), s32[]{:S(2)}) async-start(), calls=%async_computation.1 | async-start | bytes 3727360
Sparse Core Ops, SparseCore 0:
  216.7 180.1 all-reduce.3
  415.4 136.9 reduce-scatter.4
where the time goes:
time: 565 us; the launch traced here: 561 us
  blocking collectives  305 us (54%)
  waiting for transfers between devices  189 us (33%)
  matrix products  25 us (4%)
  local copies, waits for them, and re-layouts  20.4 us (4%)
  between operations  14.1 us (2%)
  other arithmetic  6.81 us (1%)
    unnamed x4, waiting for transfers between devices  189 us
    unnamed x1, blocking collectives  127 us
    pmax x1, blocking collectives, per_device(): global_max = lax.pmax(row_max, 'ctx')  124 us
    all_gather x1, blocking collectives, per_device(): full_query = lax.all_gather(own_query, 'ctx', axis=2, tiled=True)  54.8 us
    unnamed x14, local copies, waits for them, and re-layouts  17.1 us
    dot_general x1, matrix products, block_terms(): jnp.einsum('bqhc,btc->bqht', full_query, cache_block, preferred_element_t...  13.1 us
  transfers between devices with their start and end apart: 2, of which 2 were waited for; matrix products, arithmetic and copies ran while one was open for 0% of the time, Pallas kernels for 0%

commit v1 on v0

v1 whole, which is shorter than its diff:
```python
import functools
import math

import jax
import jax.numpy as jnp
from jax import lax
from jax.experimental import pallas as pl
from jax.experimental.pallas import tpu as pltpu
from jax.sharding import PartitionSpec as P

MESH = pl.DeviceIdType.MESH
F32 = jnp.float32
BF16 = jnp.bfloat16

NX, NZ, NC = 4, 8, 2
NXC = NX * NC
LAT, ROPE, NOPE, VDIM = 512, 64, 128, 128
WIDE = 640
SLOTS = 4096
PAGE = 128
D = 7168
DOUT = D // (NX * NZ * NC)
ROWS = 256
CHUNK = 1024
SIGMA = (NOPE + ROPE) ** -0.5
KAPPA = SIGMA * math.log2(math.e)
FLOOR = -1.0e30


def split3(v):
    hi = v.astype(BF16).astype(F32)
    rest = v - hi
    mid = rest.astype(BF16).astype(F32)
    return hi, mid, rest - mid


def pack_stats(c, l):
    lane = lax.broadcasted_iota(jnp.int32, c.shape, c.ndim - 1)
    out = jnp.zeros_like(c)
    for i, part in enumerate(split3(c) + split3(l)):
        out = jnp.where(lane == i, part, out)
    return out


def unpack_stats(st):
    lane = lax.broadcasted_iota(jnp.int32, st.shape, st.ndim - 1)
    c = jnp.sum(jnp.where(lane < 3, st, 0.0), axis=-1, keepdims=True)
    l = jnp.sum(jnp.where((lane >= 3) & (lane < 6), st, 0.0), axis=-1, keepdims=True)
    return c, l


def merge(parts):
    stats = [unpack_stats(p[..., LAT:]) for p in parts]
    c = stats[0][0]
    for ci, _ in stats[1:]:
        c = jnp.maximum(c, ci)
    total, l = None, None
    for p, (ci, li) in zip(parts, stats):
        f = jnp.exp2(KAPPA * (ci - c))
        term, lt = p[..., :LAT] * f, li * f
        total = term if total is None else total + term
        l = lt if l is None else l + lt
    return total, c, l


def kernel(
    q_hbm, ka_hbm, kt_hbm, page_ref, len_ref, scale_ref, rate_ref, vu_hbm, w_hbm,
    out_ref,
    q_s, x_s, ka_s, kt_s, vu_s, w_s,
    ag1, qall, s_buf, acc, rate_b, scale_b,
    rs1_send, rs1_recv, held, rs2_send, rs2_recv, o1_send, o1_recv, o2_send, o2_recv,
    local_sem, ag1_ss, ag1_rs, ag2_ss, ag2_rs, rs1_ss, rs1_rs, rs2_ss, rs2_rs,
    o1_ss, o1_rs, o2_ss, o2_rs,
):
    ctx = lax.axis_index("ctx")
    rep = lax.axis_index("rep")
    x, z, c = ctx // (NZ * NC), (ctx // NC) % NZ, ctx % NC
    xc = x * NC + c

    def z_peer(zz):
        return ((x * NZ + zz) * NC + c, rep)

    def xc_peer(o):
        return (((o // NC) * NZ + z) * NC + o % NC, rep)

    barrier = pltpu.get_barrier_semaphore()
    for k in range(1, 8):
        pl.semaphore_signal(barrier, inc=1, device_id=z_peer((z + k) % NZ), device_id_type=MESH)
        pl.semaphore_signal(barrier, inc=1, device_id=xc_peer((xc + k) % NXC), device_id_type=MESH)

    loads = [
        pltpu.make_async_copy(q_hbm, q_s, local_sem.at[0]),
        pltpu.make_async_copy(ka_hbm, ka_s, local_sem.at[1]),
        pltpu.make_async_copy(kt_hbm.at[0], kt_s.at[0, pl.ds(0, LAT + ROPE)], local_sem.at[2]),
        pltpu.make_async_copy(kt_hbm.at[1], kt_s.at[1, pl.ds(0, LAT + ROPE)], local_sem.at[3]),
        pltpu.make_async_copy(vu_hbm, vu_s, local_sem.at[4]),
        pltpu.make_async_copy(w_hbm, w_s, local_sem.at[5]),
    ]
    for load in loads:
        load.start()

    loads[0].wait()
    for r in range(2):
        for q in range(2):
            x_s[pl.ds(4 * r + 2 * q, 2), :] = q_s[r, q].astype(F32)
    loads[1].wait()
    xq = x_s[...]
    nope = xq[:, :NOPE].astype(BF16)
    lat0 = jnp.dot(nope, ka_s[0], preferred_element_type=F32)
    lat1 = jnp.dot(nope, ka_s[1], preferred_element_type=F32)
    row8 = lax.broadcasted_iota(jnp.int32, (8, LAT), 0)
    ag1[z, :, pl.ds(0, LAT)] = jnp.where(row8 % 2 == 0, lat0, lat1).astype(BF16)
    ag1[z, :, pl.ds(LAT, 128)] = jnp.zeros((8, 128), BF16)
    ag1[z, :, pl.ds(LAT, ROPE)] = xq[:, NOPE:].astype(BF16)

    pl.semaphore_wait(barrier, 14)

    def ag1_copy(k, slot):
        return pltpu.make_async_remote_copy(
            src_ref=ag1.at[slot], dst_ref=ag1.at[slot],
            send_sem=ag1_ss.at[k], recv_sem=ag1_rs.at[slot],
            device_id=z_peer((z + k) % NZ), device_id_type=MESH)

    for k in range(1, 8):
        ag1_copy(k, z).start()

    for r in range(2):
        kt_s[r, pl.ds(LAT + ROPE, 64), :] = jnp.zeros((64, SLOTS), BF16)
    row = lax.broadcasted_iota(jnp.int32, (ROWS, 128), 0)
    lane = lax.broadcasted_iota(jnp.int32, (ROWS, 128), 1)
    head = (row // 64) * 32 + ((row // 4) % 8) * 4 + ((row // 32) % 2) * 2 + row % 2
    hot = lane == head
    rate_col = jnp.sum(jnp.where(hot, rate_ref[...], 0.0), axis=-1, keepdims=True)
    scale_col = jnp.sum(jnp.where(hot, scale_ref[...], 0.0), axis=-1, keepdims=True)
    rate_b[...] = jnp.broadcast_to(rate_col, (ROWS, 128))
    scale_b[...] = jnp.broadcast_to(scale_col * (1.0 / SIGMA), (ROWS, 128))
    o1_send[...] = jnp.zeros_like(o1_send)

    for k in range(1, 8):
        ag1_copy(k, (z + k) % NZ).wait_recv()

    blocks = ag1[...].astype(F32).reshape(4, 2, 8, WIDE)
    even, odd = blocks[:, 0], blocks[:, 1]
    sub = lax.broadcasted_iota(jnp.int32, (4, 8, WIDE), 1)
    first = jnp.where(sub < 4, even, pltpu.roll(odd, 4, 1))
    second = jnp.where(sub < 4, pltpu.roll(even, 4, 1), odd)
    qall[0, xc] = first.reshape(32, WIDE).astype(BF16)
    qall[1, xc] = second.reshape(32, WIDE).astype(BF16)

    def ag2_copy(r, k, slot):
        return pltpu.make_async_remote_copy(
            src_ref=qall.at[r, slot], dst_ref=qall.at[r, slot],
            send_sem=ag2_ss.at[r, k], recv_sem=ag2_rs.at[r, slot],
            device_id=xc_peer((xc + k) % NXC), device_id_type=MESH)

    for r in range(2):
        for k in range(1, 8):
            ag2_copy(r, k, xc).start()

    sub8 = lax.broadcasted_iota(jnp.int32, (8, 128), 0)
    lane8 = lax.broadcasted_iota(jnp.int32, (8, 128), 1)
    offset = ((sub8 // 2) % 2 - lane8).astype(F32)

    def attention(r):
        full_query = qall[r].reshape(ROWS, WIDE)
        rate = rate_b[...].reshape(32, 8, 128)
        scale = scale_b[...].reshape(32, 8, 128)
        base = len_ref[r] - 2

        def scores(i, peak):
            cols = pl.ds(pl.multiple_of(i * CHUNK, CHUNK), CHUNK)
            s = jnp.dot(full_query, kt_s[r, :, cols], preferred_element_type=F32)
            for p in range(CHUNK // PAGE):
                page = page_ref[r, i * (CHUNK // PAGE) + p]
                dist = (base - page * PAGE).astype(F32) + offset
                dist = jnp.where(dist >= 0.0, dist, jnp.inf)
                bias = scale * jnp.log(1.0 + rate * dist[None])
                u = s[:, p * PAGE:(p + 1) * PAGE].reshape(32, 8, 128) - bias
                s_buf[:, pl.ds(pl.multiple_of(i * CHUNK + p * PAGE, PAGE), PAGE)] = u.reshape(ROWS, 128)
                peak = jnp.maximum(peak, u)
            return peak

        peak = lax.fori_loop(0, SLOTS // CHUNK, scores, jnp.full((32, 8, 128), FLOOR, F32))
        shift = jnp.max(peak, axis=-1, keepdims=True)
        acc[...] = jnp.zeros_like(acc)

        def sums(i, total):
            weights = []
            for p in range(CHUNK // PAGE):
                u = s_buf[:, pl.ds(pl.multiple_of(i * CHUNK + p * PAGE, PAGE), PAGE)]
                w = jnp.exp2(KAPPA * (u.reshape(32, 8, 128) - shift))
                total = total + w
                weights.append(w.reshape(ROWS, 128).astype(BF16))
            cols = pl.ds(pl.multiple_of(i * CHUNK, CHUNK), CHUNK)
            acc[...] += lax.dot_general(
                jnp.concatenate(weights, axis=1), kt_s[r, pl.ds(0, LAT), cols],
                (((1,), (1,)), ((), ())), preferred_element_type=F32)
            return total

        total = lax.fori_loop(0, SLOTS // CHUNK, sums, jnp.zeros((32, 8, 128), F32))
        total = jnp.sum(total, axis=-1, keepdims=True)
        return shift, total

    def rs1_copy(r, k, src, dst):
        return pltpu.make_async_remote_copy(
            src_ref=rs1_send.at[r, src], dst_ref=rs1_recv.at[r, dst],
            send_sem=rs1_ss.at[r, k], recv_sem=rs1_rs.at[r, dst],
            device_id=xc_peer((xc + k) % NXC), device_id_type=MESH)

    def send_partials(r, shift, total):
        stats = pack_stats(
            jnp.broadcast_to(shift, (32, 8, 128)), jnp.broadcast_to(total, (32, 8, 128)))
        rs1_send[r, :, :, pl.ds(0, LAT)] = acc[...].astype(BF16).reshape(NXC, 32, LAT)
        rs1_send[r, :, :, pl.ds(LAT, 128)] = stats.reshape(ROWS, 128).astype(BF16).reshape(NXC, 32, 128)
        for k in range(1, 8):
            rs1_copy(r, k, (xc + k) % NXC, xc).start()
        rs1_recv[r, xc] = rs1_send[r, xc]

    def merge_first(r):
        for k in range(1, 8):
            rs1_copy(r, k, xc, (xc + k) % NXC).wait_recv()
        total, shift, l = merge([rs1_recv[r, o].astype(F32).reshape(4, 8, WIDE) for o in range(NXC)])
        stats = pack_stats(jnp.broadcast_to(shift, (4, 8, 128)), jnp.broadcast_to(l, (4, 8, 128)))
        return total, stats

    loads[2].wait()
    for k in range(1, 8):
        ag2_copy(0, k, (xc + k) % NXC).wait_recv()
    send_partials(0, *attention(0))
    loads[3].wait()
    for k in range(1, 8):
        ag2_copy(1, k, (xc + k) % NXC).wait_recv()
    send_partials(1, *attention(1))

    sum0, st0 = merge_first(0)
    sum1, st1 = merge_first(1)

    for r0, r1, width, at in ((sum0, sum1, LAT, 0), (st0, st1, 128, LAT)):
        sub = lax.broadcasted_iota(jnp.int32, (4, 8, width), 1)
        even = jnp.where(sub < 4, r0, pltpu.roll(r1, 4, 1))
        odd = jnp.where(sub < 4, pltpu.roll(r0, 4, 1), r1)
        for g in range(4):
            rs2_send[2 * g, :, pl.ds(at, width)] = even[g].astype(BF16)
            rs2_send[2 * g + 1, :, pl.ds(at, width)] = odd[g].astype(BF16)

    def rs2_copy(k, src, dst):
        return pltpu.make_async_remote_copy(
            src_ref=rs2_send.at[src], dst_ref=rs2_recv.at[dst],
            send_sem=rs2_ss.at[k], recv_sem=rs2_rs.at[dst],
            device_id=z_peer((z + k) % NZ), device_id_type=MESH)

    for k in range(1, 8):
        rs2_copy(k, (z + k) % NZ, z).start()
    rs2_recv[z] = rs2_send[z]
    loads[4].wait()
    loads[5].wait()
    for k in range(1, 8):
        rs2_copy(k, z, (z + k) % NZ).wait_recv()
    total, _, l = merge([rs2_recv[o].astype(F32).reshape(1, 8, WIDE) for o in range(NZ)])
    latent = (total / l).reshape(8, LAT).astype(BF16)

    up0 = jnp.dot(latent, vu_s[0], preferred_element_type=F32)
    up1 = jnp.dot(latent, vu_s[1], preferred_element_type=F32)
    values = jnp.concatenate([up0, pltpu.roll(up1, 7, 0)], axis=1).astype(BF16)
    share = jnp.dot(values, w_s[...], preferred_element_type=F32)

    even_row = lax.broadcasted_iota(jnp.int32, (8, DOUT), 0) % 2 == 0
    for o in range(NXC):
        for g in range(4):
            j = ((o // NC) * NZ + 2 * g) * NC + o % NC
            a = share[:, j * DOUT:(j + 1) * DOUT]
            b = share[:, (j + NC) * DOUT:(j + NC + 1) * DOUT]
            o1_send[o, g, :, pl.ds(0, DOUT)] = jnp.where(even_row, a, pltpu.roll(b, 1, 0)).astype(BF16)

    def o1_copy(k, src, dst):
        return pltpu.make_async_remote_copy(
            src_ref=o1_send.at[src], dst_ref=o1_recv.at[dst],
            send_sem=o1_ss.at[k], recv_sem=o1_rs.at[dst],
            device_id=xc_peer((xc + k) % NXC), device_id_type=MESH)

    for k in range(1, 8):
        o1_copy(k, (xc + k) % NXC, xc).start()
    o1_recv[xc] = o1_send[xc]
    for k in range(1, 8):
        o1_copy(k, xc, (xc + k) % NXC).wait_recv()
    part = o1_recv[0].astype(F32)
    for o in range(1, NXC):
        part = part + o1_recv[o].astype(F32)
    o2_send[...] = part

    def o2_copy(k, src, dst):
        return pltpu.make_async_remote_copy(
            src_ref=o2_send.at[src], dst_ref=o2_recv.at[dst],
            send_sem=o2_ss.at[k], recv_sem=o2_rs.at[dst],
            device_id=z_peer((z + k) % NZ), device_id_type=MESH)

    for k in range(1, 8):
        o2_copy(k, ((z + k) % NZ) // 2, z).start()
    o2_recv[z] = o2_send[z // 2]
    for k in range(1, 8):
        o2_copy(k, 0, (z + k) % NZ).wait_recv()
    final = o2_recv[0]
    for o in range(1, NZ):
        final = final + o2_recv[o]
    final = jnp.where(z % 2 == 0, final, pltpu.roll(final, 7, 0))
    for r in range(2):
        for q in range(2):
            at = 4 * r + 2 * q
            out_ref[r, pl.ds(q, 1), :] = final[at:at + 1, :DOUT].astype(BF16)

    for k in range(1, 8):
        ag1_copy(k, z).wait_send()
        for r in range(2):
            ag2_copy(r, k, xc).wait_send()
            rs1_copy(r, k, xc, xc).wait_send()
        rs2_copy(k, z, z).wait_send()
        o1_copy(k, xc, xc).wait_send()
        o2_copy(k, 0, z).wait_send()


def per_device(queries, key_absorb, latent_cache, page_order, lengths, kerple_scale, kerple_rate,
               value_up, output_weight):
    any_spec = pl.BlockSpec(memory_space=pl.ANY)
    smem = pl.BlockSpec(memory_space=pltpu.SMEM)
    vmem = pl.BlockSpec(memory_space=pltpu.VMEM)
    dma = pltpu.SemaphoreType.DMA
    return pl.pallas_call(
        kernel,
        out_shape=jax.ShapeDtypeStruct((2, 2, DOUT), BF16),
        in_specs=[any_spec, any_spec, any_spec, smem, smem, vmem, vmem, any_spec, any_spec],
        out_specs=vmem,
        scratch_shapes=[
            pltpu.VMEM((2, 2, 2, NOPE + ROPE), BF16),
            pltpu.VMEM((8, NOPE + ROPE), F32),
            pltpu.VMEM((2, NOPE, LAT), BF16),
            pltpu.VMEM((2, WIDE, SLOTS), BF16),
            pltpu.VMEM((2, LAT, VDIM), BF16),
            pltpu.VMEM((2 * VDIM, D), BF16),
            pltpu.VMEM((NZ, 8, WIDE), BF16),
            pltpu.VMEM((2, NXC, 32, WIDE), BF16),
            pltpu.VMEM((ROWS, SLOTS), F32),
            pltpu.VMEM((ROWS, LAT), F32),
            pltpu.VMEM((ROWS, 128), F32),
            pltpu.VMEM((ROWS, 128), F32),
            pltpu.VMEM((2, NXC, 32, WIDE), BF16),
            pltpu.VMEM((2, NXC, 32, WIDE), BF16),
            pltpu.VMEM((4, 8, WIDE), F32),
            pltpu.VMEM((NZ, 8, WIDE), BF16),
            pltpu.VMEM((NZ, 8, WIDE), BF16),
            pltpu.VMEM((NXC, 4, 8, 128), BF16),
            pltpu.VMEM((NXC, 4, 8, 128), BF16),
            pltpu.VMEM((4, 8, 128), F32),
            pltpu.VMEM((NZ, 8, 128), F32),
            dma((6,)),
            dma((8,)), dma((8,)),
            dma((2, 8)), dma((2, 8)),
            dma((2, 8)), dma((2, 8)),
            dma((8,)), dma((8,)),
            dma((8,)), dma((8,)),
            dma((8,)), dma((8,)),
        ],
        compiler_params=pltpu.CompilerParams(
            collective_id=0, has_side_effects=True, vmem_limit_bytes=56 * 1024 * 1024),
    )(
        queries, key_absorb, jnp.swapaxes(latent_cache, 1, 2), page_order, lengths,
        kerple_scale.reshape(1, 128), kerple_rate.reshape(1, 128), value_up, output_weight,
    )


def solution(mesh):
    in_specs = (
        P("rep", None, "ctx", None),
        P("ctx", None, None),
        P("rep", "ctx", None),
        P("rep", "ctx"),
        P("rep"),
        P(),
        P(),
        P("ctx", None, None),
        P("ctx", None),
    )
    out_specs = P("rep", None, "ctx")
    return jax.shard_map(
        per_device, mesh=mesh, in_specs=in_specs, out_specs=out_specs, check_vma=False
    )
```

time: 565 us -> 54.3 us (0.10)
  blocking collectives: 305 us -> 0 us
  waiting for transfers between devices: 189 us -> 0 us
  Pallas kernels: 0 us -> 52.9 us
  matrix products: 25 us -> 0 us
  local copies, waits for them, and re-layouts: 20.4 us -> 1.25 us
  between operations: 14.1 us -> 0.01 us
  other arithmetic: 6.81 us -> 0 us
    unnamed x4 -> x0, waiting for transfers between devices: 189 us -> none
    unnamed x1 -> x0, blocking collectives: 127 us -> none
    pmax x1 -> x0, blocking collectives: 124 us -> none  [per_device(): global_max = lax.pmax(row_max, 'ctx')]
    all_gather x1 -> x0, blocking collectives: 54.8 us -> none  [per_device(): full_query = lax.all_gather(own_query, 'ctx', axis=2, tiled=True)]
    pallas_call x0 -> x1, Pallas kernels: none -> 52.9 us  [per_device(): pl.pallas_call(kernel, out_shape=jax.ShapeDtypeStruct((2, 2, DOUT), BF16)...]
    dot_general x5 -> x0, matrix products: 25 us -> none  [the longest x1 13.1 us: block_terms(): jnp.einsum('bqhc,btc->bqht', full_query, cache_block, preferred_element_t...]
    unnamed x14 -> x1, local copies, waits for them, and re-layouts: 17.1 us -> 1.25 us
  transfers between devices with their start and end apart: 2 -> 0, of which waited for: 2 -> 0; matrix products, arithmetic and copies ran while one was open for 0% -> 0% of each run, Pallas kernels for 0% -> 0%
where the time goes in v1:
time: 54.3 us; the launch traced here: 54.1 us
  Pallas kernels  52.9 us (97%)
  local copies, waits for them, and re-layouts  1.25 us (2%)
    pallas_call x1, Pallas kernels, per_device(): pl.pallas_call(kernel, out_shape=jax.ShapeDtypeStruct((2, 2, DOUT), BF16)...  52.9 us
    unnamed x1, local copies, waits for them, and re-layouts  1.25 us

profile of v1, /device:TPU:1, one launch (start us, length us, event | category | flops | bytes accessed | tf_op | source)
XLA Modules:
  0.0 54.1 jit_solution(9294924039584969228)
XLA Ops:
  0.0 52.9 %shard_map.91 = bf16[2,2,112]{2,1,0:T(2,128)(2,1)} custom-call(bf16[2,2,2,192]{3,2,1,0:T(2,128)(2,1)} %q_hbm.1, bf16[2,128,512]{2,1,0:T(8,128)(2,1)} %ka_hbm.1, bf16[2,576,4096]{2,1,0:T(8,128)(2,1)} %bitcast.3, s32[2,32]{1,0:T(2,128)} %page_ref.1, s32[2]{0:T(128)} %len_ref.1, f32[1,128]{1,0:T(1,128)} %bitcast.4, f32[1,128]{1,0:T(1,128)} %bitcast.5, ...), custom_call_target="tpu_custom_call" | custom-call | tf_op jit(solution)/shard_map/pallas_call | solution.py:327
  52.9 1.2 %copy.11 = bf16[2,2,112]{2,1,0:T(2,128)(2,1)} copy(bf16[2,2,112]{2,1,0:T(2,128)(2,1)} %shard_map.91) | data formatting | bytes 1792

commit v2 on v0

v2 whole, which is shorter than its diff:
```python
import functools
import math

import jax
import jax.numpy as jnp
from jax import lax
from jax.experimental import pallas as pl
from jax.experimental.pallas import tpu as pltpu
from jax.sharding import PartitionSpec as P

MESH = pl.DeviceIdType.MESH
F32 = jnp.float32
BF16 = jnp.bfloat16

NX, NZ, NC = 4, 8, 2
LAT, ROPE, NOPE, VDIM = 512, 64, 128, 128
WIDE = 640
SLOTS = 4096
PAGE = 128
D = 7168
DOUT = D // (NX * NZ * NC)
ROWS = 256
HALF = ROWS // 2
NCHIP = NX * NZ
CHUNK = 1024
SIGMA = (NOPE + ROPE) ** -0.5
KAPPA = SIGMA * math.log2(math.e)
FLOOR = -1.0e30


AWAY = sorted(
    ((dx, dz) for dx in range(NX) for dz in range(NZ) if dx or dz),
    key=lambda d: -min(d[0], NX - d[0]) - min(d[1], NZ - d[1]))


def split3(v):
    hi = v.astype(BF16).astype(F32)
    rest = v - hi
    mid = rest.astype(BF16).astype(F32)
    return hi, mid, rest - mid


def pack_stats(c, l):
    lane = lax.broadcasted_iota(jnp.int32, c.shape, c.ndim - 1)
    out = jnp.zeros_like(c)
    for i, part in enumerate(split3(c) + split3(l)):
        out = jnp.where(lane == i, part, out)
    return out


def unpack_stats(st):
    lane = lax.broadcasted_iota(jnp.int32, st.shape, st.ndim - 1)
    c = jnp.sum(jnp.where(lane < 3, st, 0.0), axis=-1, keepdims=True)
    l = jnp.sum(jnp.where((lane >= 3) & (lane < 6), st, 0.0), axis=-1, keepdims=True)
    return c, l


def kernel(
    q_hbm, ka_hbm, kt_hbm, page_hbm, len_hbm, scale_hbm, rate_hbm, vu_hbm, w_hbm,
    out_ref,
    q_s, x_s, ka_s, kt_s, page_s, len_s, scale_s, rate_s, vu_s, w_s,
    qin, qf, qall, s_buf, acc, rate_b, scale_b,
    pair_send, pair_recv, rs_f, rs_send, rs_recv, lat_s, o_pair, o_pair_recv, o_send, o_recv,
    local_sem, ag_ss, ag_rs, relay_ss, relay_rs, pair_ss, pair_rs, rs_ss, rs_rs,
    op_ss, op_rs, o_ss, o_rs,
):
    ctx = lax.axis_index("ctx")
    rep = lax.axis_index("rep")
    chip, c = ctx // NC, ctx % NC
    x, z = chip // NZ, chip % NZ
    sibling = (chip * NC + 1 - c, rep)

    def away_chip(d):
        return ((x + d[0]) % NX) * NZ + (z + d[1]) % NZ

    def away(d):
        return (away_chip(d) * NC + c, rep)

    barrier = pltpu.get_barrier_semaphore()
    for d in AWAY:
        pl.semaphore_signal(barrier, inc=1, device_id=away(d), device_id_type=MESH)
    pl.semaphore_signal(barrier, inc=1, device_id=sibling, device_id_type=MESH)

    loads = {
        name: pltpu.make_async_copy(src, dst, local_sem.at[i])
        for i, (name, src, dst) in enumerate((
            ("q", q_hbm, q_s),
            ("ka", ka_hbm, ka_s),
            ("scale", scale_hbm, scale_s),
            ("rate", rate_hbm, rate_s),
            ("page", page_hbm, page_s),
            ("len", len_hbm, len_s),
            ("k0", kt_hbm.at[0], kt_s.at[0, pl.ds(0, LAT + ROPE)]),
            ("k1", kt_hbm.at[1], kt_s.at[1, pl.ds(0, LAT + ROPE)]),
            ("vu", vu_hbm, vu_s),
            ("w", w_hbm, w_s),
        ))
    }
    for load in loads.values():
        load.start()

    loads["q"].wait()
    for r in range(2):
        for q in range(2):
            for hh in range(2):
                x_s[pl.ds(4 * r + 2 * hh + q, 1), :] = q_s[r, q, pl.ds(hh, 1), :].astype(F32)
    loads["ka"].wait()
    xq = x_s[...]
    nope = xq[:, :NOPE].astype(BF16)
    lat0 = jnp.dot(nope, ka_s[0], preferred_element_type=F32)
    lat1 = jnp.dot(nope, ka_s[1], preferred_element_type=F32)
    row8 = lax.broadcasted_iota(jnp.int32, (8, LAT), 0)
    lat = jnp.where((row8 // 2) % 2 == 0, lat0, lat1)
    for r in range(2):
        qin[r, chip, :, pl.ds(0, LAT)] = lat[4 * r:4 * r + 4].astype(BF16)
        qin[r, chip, :, pl.ds(LAT, 128)] = jnp.zeros((4, 128), BF16)
        qin[r, chip, :, pl.ds(LAT, ROPE)] = xq[4 * r:4 * r + 4, NOPE:].astype(BF16)

    pl.semaphore_wait(barrier, len(AWAY) + 1)

    def ag_copy(r, d):
        return pltpu.make_async_remote_copy(
            src_ref=qin.at[r, chip], dst_ref=qin.at[r, chip],
            send_sem=ag_ss.at[r], recv_sem=ag_rs.at[r],
            device_id=away(d), device_id_type=MESH)

    def ag_all(r):
        return pltpu.make_async_remote_copy(
            src_ref=qin.at[r, pl.ds(0, NCHIP - 1)], dst_ref=qin.at[r, pl.ds(0, NCHIP - 1)],
            send_sem=ag_ss.at[r], recv_sem=ag_rs.at[r],
            device_id=sibling, device_id_type=MESH)

    for r in range(2):
        for d in AWAY:
            ag_copy(r, d).start()

    for r in range(2):
        kt_s[r, pl.ds(LAT + ROPE, 64), :] = jnp.zeros((64, SLOTS), BF16)
    o_pair[...] = jnp.zeros_like(o_pair)
    row = lax.broadcasted_iota(jnp.int32, (ROWS, 128), 0)
    lane = lax.broadcasted_iota(jnp.int32, (ROWS, 128), 1)
    head = ((row // 4) % 32) * 4 + (row // 128) * 2 + (row // 2) % 2
    hot = lane == head
    loads["scale"].wait()
    loads["rate"].wait()
    rate_col = jnp.sum(jnp.where(hot, rate_s[...], 0.0), axis=-1, keepdims=True)
    scale_col = jnp.sum(jnp.where(hot, scale_s[...], 0.0), axis=-1, keepdims=True)
    rate_b[...] = jnp.broadcast_to(rate_col, (ROWS, 128))
    scale_b[...] = jnp.broadcast_to(scale_col * (1.0 / SIGMA), (ROWS, 128))
    loads["page"].wait()
    loads["len"].wait()

    def relay_copy(r, half):
        return pltpu.make_async_remote_copy(
            src_ref=qall.at[r, half], dst_ref=qall.at[r, half],
            send_sem=relay_ss.at[r], recv_sem=relay_rs.at[r],
            device_id=sibling, device_id_type=MESH)

    def relay(r):
        ag_all(r).wait_recv()
        for i in range(NCHIP // 2):
            qf[pl.ds(8 * i, 4), :] = qin[r, 2 * i].astype(F32)
            qf[pl.ds(8 * i + 4, 4), :] = qin[r, 2 * i + 1].astype(F32)
        qall[r, c] = qf[...].astype(BF16)
        relay_copy(r, c).start()

    sub8 = lax.broadcasted_iota(jnp.int32, (8, 128), 0)
    lane8 = lax.broadcasted_iota(jnp.int32, (8, 128), 1)
    offset = (sub8 % 2 - lane8).astype(F32)

    def scores(r, first, last, peak):
        full_query = qall[r].reshape(ROWS, WIDE)
        rate = rate_b[...].reshape(32, 8, 128)
        scale = scale_b[...].reshape(32, 8, 128)
        base = len_s[r] - 2

        def step(i, peak):
            cols = pl.ds(pl.multiple_of(i * CHUNK, CHUNK), CHUNK)
            s = jnp.dot(full_query, kt_s[r, :, cols], preferred_element_type=F32)
            for p in range(CHUNK // PAGE):
                page = page_s[r, i * (CHUNK // PAGE) + p]
                dist = (base - page * PAGE).astype(F32) + offset
                dist = jnp.where(dist >= 0.0, dist, jnp.inf)
                bias = scale * jnp.log(1.0 + rate * dist[None])
                u = s[:, p * PAGE:(p + 1) * PAGE].reshape(32, 8, 128) - bias
                s_buf[:, pl.ds(pl.multiple_of(i * CHUNK + p * PAGE, PAGE), PAGE)] = u.reshape(ROWS, 128)
                peak = jnp.maximum(peak, u)
            return peak

        return lax.fori_loop(first, last, step, peak)

    def sums(r, shift):
        acc[...] = jnp.zeros_like(acc)

        def step(i, total):
            weights = []
            for p in range(CHUNK // PAGE):
                u = s_buf[:, pl.ds(pl.multiple_of(i * CHUNK + p * PAGE, PAGE), PAGE)]
                w = jnp.exp2(KAPPA * (u.reshape(32, 8, 128) - shift))
                total = total + w
                weights.append(w.reshape(ROWS, 128).astype(BF16))
            cols = pl.ds(pl.multiple_of(i * CHUNK, CHUNK), CHUNK)
            acc[...] += lax.dot_general(
                jnp.concatenate(weights, axis=1), kt_s[r, pl.ds(0, LAT), cols],
                (((1,), (1,)), ((), ())), preferred_element_type=F32)
            return total

        total = lax.fori_loop(0, SLOTS // CHUNK, step, jnp.zeros((32, 8, 128), F32))
        return jnp.sum(total, axis=-1, keepdims=True)

    def pair_copy(r):
        return pltpu.make_async_remote_copy(
            src_ref=pair_send.at[r], dst_ref=pair_recv.at[r],
            send_sem=pair_ss.at[r], recv_sem=pair_rs.at[r],
            device_id=sibling, device_id_type=MESH)

    def rows_of(core):
        return pl.ds(pl.multiple_of(core * HALF, HALF), HALF)

    def send_pair(r, shift, total):
        stats = pack_stats(
            jnp.broadcast_to(shift, (32, 8, 128)), jnp.broadcast_to(total, (32, 8, 128)))
        stats = stats.reshape(2, HALF, 128)
        pair_send[r, :, pl.ds(0, LAT)] = acc[rows_of(1 - c), :].astype(BF16)
        pair_send[r, :, pl.ds(LAT, 128)] = jnp.where(c == 0, stats[1], stats[0]).astype(BF16)
        pair_copy(r).start()
        rs_f[:, pl.ds(0, LAT)] = acc[rows_of(c), :]
        rs_f[:, pl.ds(LAT, 128)] = jnp.where(c == 0, stats[0], stats[1])

    def rs_copy(r, d):
        return pltpu.make_async_remote_copy(
            src_ref=rs_send.at[r, away_chip(d)], dst_ref=rs_recv.at[r, chip],
            send_sem=rs_ss.at[r], recv_sem=rs_rs.at[r],
            device_id=away(d), device_id_type=MESH)

    def rs_all(r):
        return pltpu.make_async_remote_copy(
            src_ref=rs_send.at[r, pl.ds(0, NCHIP - 1)], dst_ref=rs_recv.at[r, pl.ds(0, NCHIP - 1)],
            send_sem=rs_ss.at[r], recv_sem=rs_rs.at[r],
            device_id=sibling, device_id_type=MESH)

    def send_rows(r):
        pair_copy(r).wait_recv()
        mine = rs_f[...].reshape(16, 8, WIDE)
        theirs = pair_recv[r].astype(F32).reshape(16, 8, WIDE)
        (c0, l0), (c1, l1) = unpack_stats(mine[..., LAT:]), unpack_stats(theirs[..., LAT:])
        shift = jnp.maximum(c0, c1)
        f0, f1 = jnp.exp2(KAPPA * (c0 - shift)), jnp.exp2(KAPPA * (c1 - shift))
        both = mine[..., :LAT] * f0 + theirs[..., :LAT] * f1
        stats = pack_stats(
            jnp.broadcast_to(shift, (16, 8, 128)), jnp.broadcast_to(l0 * f0 + l1 * f1, (16, 8, 128)))
        for i in range(NCHIP // 2):
            for h in range(2):
                rs_send[r, 2 * i + h, :, pl.ds(0, LAT)] = both[i, 4 * h:4 * h + 4].astype(BF16)
                rs_send[r, 2 * i + h, :, pl.ds(LAT, 128)] = stats[i, 4 * h:4 * h + 4].astype(BF16)
        for d in AWAY:
            rs_copy(r, d).start()
        rs_recv[r, chip] = rs_send[r, chip]

    def finish_rows(r):
        rs_all(r).wait_recv()
        parts = rs_recv[r].astype(F32)
        ci, li = unpack_stats(parts[..., LAT:])
        f = jnp.exp2(KAPPA * (ci - jnp.max(ci, axis=0, keepdims=True)))
        total = jnp.sum(parts[..., :LAT] * f, axis=0)
        lat_s[pl.ds(4 * r, 4), :] = total / jnp.sum(li * f, axis=0)

    def start_peak():
        return jnp.full((32, 8, 128), FLOOR, F32)

    n = SLOTS // CHUNK
    relay(0)
    loads["k0"].wait()
    relay_copy(0, 1 - c).wait_recv()
    shift = jnp.max(scores(0, 0, n, start_peak()), axis=-1, keepdims=True)
    relay(1)
    send_pair(0, shift, sums(0, shift))
    loads["k1"].wait()
    relay_copy(1, 1 - c).wait_recv()
    peak = scores(1, 0, n // 2, start_peak())
    send_rows(0)
    shift = jnp.max(scores(1, n // 2, n, peak), axis=-1, keepdims=True)
    send_pair(1, shift, sums(1, shift))
    send_rows(1)
    loads["vu"].wait()
    loads["w"].wait()
    finish_rows(0)
    finish_rows(1)

    latent = lat_s[...].astype(BF16)
    up0 = jnp.dot(latent, vu_s[0], preferred_element_type=F32)
    up1 = jnp.dot(latent, vu_s[1], preferred_element_type=F32)
    values = jnp.concatenate([up0, pltpu.roll(up1, 6, 0)], axis=1)
    row8 = lax.broadcasted_iota(jnp.int32, values.shape, 0)
    values = jnp.where(row8 < 2, values, pltpu.roll(values, 6, 0)).astype(BF16)
    share = jnp.dot(values, w_s[...], preferred_element_type=F32)
    for j in range(NCHIP * NC):
        o_pair[j % NC, j // NC, :, pl.ds(0, DOUT)] = share[:4, j * DOUT:(j + 1) * DOUT]

    pair_out = pltpu.make_async_remote_copy(
        src_ref=o_pair.at[1 - c], dst_ref=o_pair_recv,
        send_sem=op_ss, recv_sem=op_rs, device_id=sibling, device_id_type=MESH)
    pair_out.start()
    pair_out.wait_recv()
    o_send[...] = (o_pair[c] + o_pair_recv[...]).astype(BF16)

    def o_copy(d):
        return pltpu.make_async_remote_copy(
            src_ref=o_send.at[away_chip(d)], dst_ref=o_recv.at[chip],
            send_sem=o_ss, recv_sem=o_rs, device_id=away(d), device_id_type=MESH)

    o_all = pltpu.make_async_remote_copy(
        src_ref=o_send.at[pl.ds(0, NCHIP - 1)], dst_ref=o_recv.at[pl.ds(0, NCHIP - 1)],
        send_sem=o_ss, recv_sem=o_rs, device_id=sibling, device_id_type=MESH)
    for d in AWAY:
        o_copy(d).start()
    o_recv[chip] = o_send[chip]
    o_all.wait_recv()
    final = jnp.sum(o_recv[...].astype(F32), axis=0)
    for r in range(2):
        for q in range(2):
            at = 2 * r + q
            out_ref[r, pl.ds(q, 1), :] = final[at:at + 1, :DOUT]

    for r in range(2):
        ag_all(r).wait_send()
        relay_copy(r, c).wait_send()
        pair_copy(r).wait_send()
        rs_all(r).wait_send()
    pair_out.wait_send()
    o_all.wait_send()


def per_device(queries, key_absorb, latent_cache, page_order, lengths, kerple_scale, kerple_rate,
               value_up, output_weight):
    any_spec = pl.BlockSpec(memory_space=pl.ANY)
    dma = pltpu.SemaphoreType.DMA
    out = pl.pallas_call(
        kernel,
        out_shape=jax.ShapeDtypeStruct((2, 2, DOUT), F32),
        in_specs=[any_spec] * 9,
        out_specs=pl.BlockSpec(memory_space=pltpu.VMEM),
        scratch_shapes=[
            pltpu.VMEM((2, 2, 2, NOPE + ROPE), BF16),
            pltpu.VMEM((8, NOPE + ROPE), F32),
            pltpu.VMEM((2, NOPE, LAT), BF16),
            pltpu.VMEM((2, WIDE, SLOTS), BF16),
            pltpu.SMEM((2, SLOTS // PAGE), jnp.int32),
            pltpu.SMEM((2,), jnp.int32),
            pltpu.VMEM((1, 128), F32),
            pltpu.VMEM((1, 128), F32),
            pltpu.VMEM((2, LAT, VDIM), BF16),
            pltpu.VMEM((2 * VDIM, D), BF16),
            pltpu.VMEM((2, NCHIP, 4, WIDE), BF16),
            pltpu.VMEM((HALF, WIDE), F32),
            pltpu.VMEM((2, NC, HALF, WIDE), BF16),
            pltpu.VMEM((ROWS, SLOTS), F32),
            pltpu.VMEM((ROWS, LAT), F32),
            pltpu.VMEM((ROWS, 128), F32),
            pltpu.VMEM((ROWS, 128), F32),
            pltpu.VMEM((2, HALF, WIDE), BF16),
            pltpu.VMEM((2, HALF, WIDE), BF16),
            pltpu.VMEM((HALF, WIDE), F32),
            pltpu.VMEM((2, NCHIP, 4, WIDE), BF16),
            pltpu.VMEM((2, NCHIP, 4, WIDE), BF16),
            pltpu.VMEM((8, LAT), F32),
            pltpu.VMEM((NC, NCHIP, 4, 128), F32),
            pltpu.VMEM((NCHIP, 4, 128), F32),
            pltpu.VMEM((NCHIP, 4, 128), BF16),
            pltpu.VMEM((NCHIP, 4, 128), BF16),
            dma((10,)),
            dma((2,)), dma((2,)),
            dma((2,)), dma((2,)),
            dma((2,)), dma((2,)),
            dma((2,)), dma((2,)),
            dma, dma,
            dma, dma,
        ],
        compiler_params=pltpu.CompilerParams(
            collective_id=0, has_side_effects=True, vmem_limit_bytes=56 * 1024 * 1024),
    )(
        queries, key_absorb, jnp.swapaxes(latent_cache, 1, 2), page_order, lengths,
        kerple_scale.reshape(1, 128), kerple_rate.reshape(1, 128), value_up, output_weight,
    )
    return out.astype(BF16)


def solution(mesh):
    in_specs = (
        P("rep", None, "ctx", None),
        P("ctx", None, None),
        P("rep", "ctx", None),
        P("rep", "ctx"),
        P("rep"),
        P(),
        P(),
        P("ctx", None, None),
        P("ctx", None),
    )
    out_specs = P("rep", None, "ctx")
    return jax.shard_map(
        per_device, mesh=mesh, in_specs=in_specs, out_specs=out_specs, check_vma=False
    )
```

time: 565 us -> 47.7 us (0.08)
  blocking collectives: 305 us -> 0 us
  waiting for transfers between devices: 189 us -> 0 us
  Pallas kernels: 0 us -> 46.4 us
  matrix products: 25 us -> 0 us
  local copies, waits for them, and re-layouts: 20.4 us -> 0 us
  between operations: 14.1 us -> 0.01 us
    unnamed x4 -> x0, waiting for transfers between devices: 189 us -> none
    unnamed x1 -> x0, blocking collectives: 127 us -> none
    pmax x1 -> x0, blocking collectives: 124 us -> none  [per_device(): global_max = lax.pmax(row_max, 'ctx')]
    all_gather x1 -> x0, blocking collectives: 54.8 us -> none  [per_device(): full_query = lax.all_gather(own_query, 'ctx', axis=2, tiled=True)]
    pallas_call x0 -> x1, Pallas kernels: none -> 46.4 us  [per_device(): pl.pallas_call(kernel, out_shape=jax.ShapeDtypeStruct((2, 2, DOUT), F32),...]
    dot_general x5 -> x0, matrix products: 25 us -> none  [the longest x1 13.1 us: block_terms(): jnp.einsum('bqhc,btc->bqht', full_query, cache_block, preferred_element_t...]
    unnamed x14 -> x0, local copies, waits for them, and re-layouts: 17.1 us -> none
  transfers between devices with their start and end apart: 2 -> 0, of which waited for: 2 -> 0; matrix products, arithmetic and copies ran while one was open for 0% -> 0% of each run, Pallas kernels for 0% -> 0%
where the time goes in v2:
time: 47.7 us; the launch traced here: 47.6 us
  Pallas kernels  46.4 us (97%)
  other arithmetic  1.25 us (3%)
    pallas_call x1, Pallas kernels, per_device(): pl.pallas_call(kernel, out_shape=jax.ShapeDtypeStruct((2, 2, DOUT), F32),...  46.4 us
    convert_element_type x1, other arithmetic, per_device(): return out.astype(BF16)  1.25 us

profile of v2, /device:TPU:1, one launch (start us, length us, event | category | flops | bytes accessed | tf_op | source)
XLA Modules:
  0.0 47.6 jit_solution(14558311616900915606)
XLA Ops:
  0.0 46.4 %shard_map.91 = f32[2,2,112]{2,1,0:T(2,128)} custom-call(bf16[2,2,2,192]{3,2,1,0:T(2,128)(2,1)} %q_hbm.1, bf16[2,128,512]{2,1,0:T(8,128)(2,1)} %ka_hbm.1, bf16[2,576,4096]{2,1,0:T(8,128)(2,1)} %bitcast.3, s32[2,32]{1,0:T(2,128)} %page_hbm.1, s32[2]{0:T(128)} %len_hbm.1, f32[1,128]{1,0:T(1,128)} %bitcast.4, f32[1,128]{1,0:T(1,128)} %bitcast.5, ...), custom_call_target="tpu_custom_call" | custom-call | tf_op jit(solution)/shard_map/pallas_call | solution.py:338
  46.4 1.2 %convert_element_type.3 = bf16[2,2,112]{2,1,0:T(2,128)(2,1)} convert(f32[2,2,112]{2,1,0:T(2,128)} %shard_map.91) | non-fusion elementwise | flops 448 | bytes 2688 | tf_op jit(solution)/shard_map/convert_element_type | solution.py:385

commit v3 on v2

v3 whole, which is shorter than its diff:
```python
import functools
import math

import jax
import jax.numpy as jnp
from jax import lax
from jax.experimental import pallas as pl
from jax.experimental.pallas import tpu as pltpu
from jax.sharding import PartitionSpec as P

MESH = pl.DeviceIdType.MESH
F32 = jnp.float32
BF16 = jnp.bfloat16

NX, NZ, NC = 4, 8, 2
LAT, ROPE, NOPE, VDIM = 512, 64, 128, 128
WIDE = 640
SLOTS = 4096
PAGE = 128
D = 7168
DOUT = D // (NX * NZ * NC)
ROWS = 256
HALF = ROWS // 2
NCHIP = NX * NZ
SIGMA = (NOPE + ROPE) ** -0.5
KAPPA = SIGMA * math.log2(math.e)
FLOOR = -1.0e30


def steps(slot):
    return slot % NX, (slot // NX + NZ - 1) % NZ


def hops(slot):
    dx, dz = steps(slot)
    return min(dx, NX - dx) + min(dz, NZ - dz)


SELF = NX
AWAY = sorted((t for t in range(NCHIP) if t != SELF), key=lambda t: -hops(t))
FAR_FIRST_Z = (4, 3, 5, 2, 6, 1, 7, 0)
XCOLS = D // NX


def split3(v):
    hi = v.astype(BF16).astype(F32)
    rest = v - hi
    mid = rest.astype(BF16).astype(F32)
    return hi, mid, rest - mid


def pack_stats(c, l):
    lane = lax.broadcasted_iota(jnp.int32, c.shape, c.ndim - 1)
    out = jnp.zeros_like(c)
    for i, part in enumerate(split3(c) + split3(l)):
        out = jnp.where(lane == i, part, out)
    return out


def unpack_stats(st):
    lane = lax.broadcasted_iota(jnp.int32, st.shape, st.ndim - 1)
    c = jnp.sum(jnp.where(lane < 3, st, 0.0), axis=-1, keepdims=True)
    l = jnp.sum(jnp.where((lane >= 3) & (lane < 6), st, 0.0), axis=-1, keepdims=True)
    return c, l


def kernel(
    q_hbm, ka_hbm, kt_hbm, page_hbm, len_hbm, scale_hbm, rate_hbm, vu_hbm, w_hbm,
    out_ref,
    q_s, x_s, ka_s, kt_s, page_s, len_s, scale_s, rate_s, vu_s, w_s,
    qin, qf, qall, s_buf, rate_b, scale_b,
    pair_send, pair_recv, rs_f, rs_send, rs_recv, lat_s, o_pair, o_pair_recv, o_send, o_recv,
    local_sem, ag_ss, ag_rs, relay_ss, relay_rs, pair_ss, pair_rs, rs_ss, rs_rs,
    op_ss, op_rs, o_ss, o_rs,
):
    ctx = lax.axis_index("ctx")
    rep = lax.axis_index("rep")
    chip, c = ctx // NC, ctx % NC
    x, z = chip // NZ, chip % NZ
    sibling = (chip * NC + 1 - c, rep)

    def device(dx, dz):
        return ((((x + dx) % NX) * NZ + (z + dz) % NZ) * NC + c, rep)

    def toward(t):
        dx, dz = steps(t)
        return device(dx, dz)

    def back(t):
        dx, dz = steps(t)
        return device(NX - dx, NZ - dz)

    barrier = pltpu.get_barrier_semaphore()
    for t in AWAY:
        pl.semaphore_signal(barrier, inc=1, device_id=toward(t), device_id_type=MESH)
    pl.semaphore_signal(barrier, inc=1, device_id=sibling, device_id_type=MESH)

    loads = {
        name: pltpu.make_async_copy(src, dst, local_sem.at[i])
        for i, (name, src, dst) in enumerate((
            ("q", q_hbm, q_s),
            ("ka", ka_hbm, ka_s),
            ("scale", scale_hbm, scale_s),
            ("rate", rate_hbm, rate_s),
            ("page", page_hbm, page_s),
            ("len", len_hbm, len_s),
            ("k0", kt_hbm.at[0], kt_s.at[0, pl.ds(0, LAT + ROPE)]),
            ("k1", kt_hbm.at[1], kt_s.at[1, pl.ds(0, LAT + ROPE)]),
            ("vu", vu_hbm, vu_s),
            ("w", w_hbm, w_s),
        ))
    }
    for load in loads.values():
        load.start()

    loads["q"].wait()
    for r in range(2):
        for q in range(2):
            for hh in range(2):
                x_s[pl.ds(4 * r + 2 * hh + q, 1), :] = q_s[r, q, pl.ds(hh, 1), :].astype(F32)
    loads["ka"].wait()
    xq = x_s[...]
    nope = xq[:, :NOPE].astype(BF16)
    lat0 = jnp.dot(nope, ka_s[0], preferred_element_type=F32)
    lat1 = jnp.dot(nope, ka_s[1], preferred_element_type=F32)
    row8 = lax.broadcasted_iota(jnp.int32, (8, LAT), 0)
    lat = jnp.where((row8 // 2) % 2 == 0, lat0, lat1)
    for r in range(2):
        qin[r, SELF, :, pl.ds(0, LAT)] = lat[4 * r:4 * r + 4].astype(BF16)
        qin[r, SELF, :, pl.ds(LAT, 128)] = jnp.zeros((4, 128), BF16)
        qin[r, SELF, :, pl.ds(LAT, ROPE)] = xq[4 * r:4 * r + 4, NOPE:].astype(BF16)

    pl.semaphore_wait(barrier, len(AWAY) + 1)

    def ag_copy(r, t):
        return pltpu.make_async_remote_copy(
            src_ref=qin.at[r, SELF], dst_ref=qin.at[r, t],
            send_sem=ag_ss.at[r, t // 16], recv_sem=ag_rs.at[r, t // 16],
            device_id=toward(t), device_id_type=MESH)

    def ag_all(r, b):
        some = qin.at[r, pl.ds(0, 15 if b == 0 else 16)]
        return pltpu.make_async_remote_copy(
            src_ref=some, dst_ref=some, send_sem=ag_ss.at[r, b], recv_sem=ag_rs.at[r, b],
            device_id=sibling, device_id_type=MESH)

    for b in range(2):
        for r in range(2):
            for t in AWAY:
                if t // 16 == b:
                    ag_copy(r, t).start()

    for r in range(2):
        kt_s[r, pl.ds(LAT + ROPE, 64), :] = jnp.zeros((64, SLOTS), BF16)
    o_pair[...] = jnp.zeros_like(o_pair)
    row = lax.broadcasted_iota(jnp.int32, (ROWS, 128), 0)
    lane = lax.broadcasted_iota(jnp.int32, (ROWS, 128), 1)
    slot = (row // 128) * 16 + (row // 4) % 16
    from_x = (x + NX - slot % NX) % NX
    from_z = (z + 2 * NZ - (slot // NX + NZ - 1)) % NZ
    core = (c + (row // 64) % 2) % NC
    head = ((from_x * NZ + from_z) * NC + core) * 2 + (row // 2) % 2
    hot = lane == head
    loads["scale"].wait()
    loads["rate"].wait()
    rate_col = jnp.sum(jnp.where(hot, rate_s[...], 0.0), axis=-1, keepdims=True)
    scale_col = jnp.sum(jnp.where(hot, scale_s[...], 0.0), axis=-1, keepdims=True)
    rate_b[...] = jnp.broadcast_to(rate_col, (ROWS, 128))
    scale_b[...] = jnp.broadcast_to(scale_col * (1.0 / SIGMA), (ROWS, 128))
    loads["page"].wait()
    loads["len"].wait()

    def relay_copy(r, b):
        return pltpu.make_async_remote_copy(
            src_ref=qall.at[r, b, 0], dst_ref=qall.at[r, b, 1],
            send_sem=relay_ss.at[r, b], recv_sem=relay_rs.at[r, b],
            device_id=sibling, device_id_type=MESH)

    def relay(r, b):
        ag_all(r, b).wait_recv()
        for i in range(8):
            qf[pl.ds(8 * i, 4), :] = qin[r, 16 * b + 2 * i].astype(F32)
            qf[pl.ds(8 * i + 4, 4), :] = qin[r, 16 * b + 2 * i + 1].astype(F32)
        qall[r, b, 0] = qf[...].astype(BF16)
        relay_copy(r, b).start()

    sub8 = lax.broadcasted_iota(jnp.int32, (8, 128), 0)
    lane8 = lax.broadcasted_iota(jnp.int32, (8, 128), 1)
    offset = (sub8 % 2 - lane8).astype(F32)

    def scores(r, b):
        relay_copy(r, b).wait_recv()
        rows = pl.ds(HALF * b, HALF)
        rate = rate_b[rows, :].reshape(16, 8, 128)
        scale = scale_b[rows, :].reshape(16, 8, 128)
        base = len_s[r] - 2
        s = jnp.dot(qall[r, b].reshape(HALF, WIDE), kt_s[r], preferred_element_type=F32)
        peak = jnp.full((16, 8, 128), FLOOR, F32)
        for p in range(SLOTS // PAGE):
            dist = (base - page_s[r, p] * PAGE).astype(F32) + offset
            dist = jnp.where(dist >= 0.0, dist, jnp.inf)
            bias = scale * jnp.log(1.0 + rate * dist[None])
            u = s[:, p * PAGE:(p + 1) * PAGE].reshape(16, 8, 128) - bias
            s_buf[r, rows, pl.ds(p * PAGE, PAGE)] = u.reshape(HALF, 128)
            peak = jnp.maximum(peak, u)
        return jnp.max(peak, axis=-1, keepdims=True)

    def sums(r, near, far):
        shift = jnp.concatenate([near, far], axis=0)
        total = jnp.zeros((32, 8, 128), F32)
        weights = []
        for p in range(SLOTS // PAGE):
            u = s_buf[r, :, pl.ds(p * PAGE, PAGE)].reshape(32, 8, 128)
            w = jnp.exp2(KAPPA * (u - shift))
            total = total + w
            weights.append(w.reshape(ROWS, 128).astype(BF16))
        summed = lax.dot_general(
            jnp.concatenate(weights, axis=1), kt_s[r, pl.ds(0, LAT), :],
            (((1,), (1,)), ((), ())), preferred_element_type=F32)
        return shift, jnp.sum(total, axis=-1, keepdims=True), summed

    def pair_copy(r):
        return pltpu.make_async_remote_copy(
            src_ref=pair_send.at[r], dst_ref=pair_recv.at[r],
            send_sem=pair_ss.at[r], recv_sem=pair_rs.at[r],
            device_id=sibling, device_id_type=MESH)

    def send_pair(r, shift, total, summed):
        stats = pack_stats(
            jnp.broadcast_to(shift, (32, 8, 128)), jnp.broadcast_to(total, (32, 8, 128)))
        stats = stats.reshape(2, 2, 64, 128)
        summed = summed.reshape(2, 2, 64, LAT)
        for b in range(2):
            rows = pl.ds(64 * b, 64)
            pair_send[r, rows, pl.ds(0, LAT)] = summed[b, 1].astype(BF16)
            pair_send[r, rows, pl.ds(LAT, 128)] = stats[b, 1].astype(BF16)
        pair_copy(r).start()
        for b in range(2):
            rows = pl.ds(64 * b, 64)
            rs_f[rows, pl.ds(0, LAT)] = summed[b, 0]
            rs_f[rows, pl.ds(LAT, 128)] = stats[b, 0]

    def rs_copy(r, t):
        return pltpu.make_async_remote_copy(
            src_ref=rs_send.at[r, t], dst_ref=rs_recv.at[r, t],
            send_sem=rs_ss.at[r], recv_sem=rs_rs.at[r],
            device_id=back(t), device_id_type=MESH)

    def rs_all(r):
        return pltpu.make_async_remote_copy(
            src_ref=rs_send.at[r, pl.ds(0, NCHIP - 1)], dst_ref=rs_recv.at[r, pl.ds(0, NCHIP - 1)],
            send_sem=rs_ss.at[r], recv_sem=rs_rs.at[r],
            device_id=sibling, device_id_type=MESH)

    def send_rows(r):
        pair_copy(r).wait_recv()
        mine = rs_f[...].reshape(16, 8, WIDE)
        theirs = pair_recv[r].astype(F32).reshape(16, 8, WIDE)
        (c0, l0), (c1, l1) = unpack_stats(mine[..., LAT:]), unpack_stats(theirs[..., LAT:])
        shift = jnp.maximum(c0, c1)
        f0, f1 = jnp.exp2(KAPPA * (c0 - shift)), jnp.exp2(KAPPA * (c1 - shift))
        both = mine[..., :LAT] * f0 + theirs[..., :LAT] * f1
        stats = pack_stats(
            jnp.broadcast_to(shift, (16, 8, 128)), jnp.broadcast_to(l0 * f0 + l1 * f1, (16, 8, 128)))
        for i in range(NCHIP // 2):
            for h in range(2):
                rs_send[r, 2 * i + h, :, pl.ds(0, LAT)] = both[i, 4 * h:4 * h + 4].astype(BF16)
                rs_send[r, 2 * i + h, :, pl.ds(LAT, 128)] = stats[i, 4 * h:4 * h + 4].astype(BF16)
        for t in AWAY:
            rs_copy(r, t).start()
        rs_recv[r, SELF] = rs_send[r, SELF]

    def finish_rows(r):
        rs_all(r).wait_recv()
        parts = rs_recv[r].astype(F32)
        ci, li = unpack_stats(parts[..., LAT:])
        f = jnp.exp2(KAPPA * (ci - jnp.max(ci, axis=0, keepdims=True)))
        total = jnp.sum(parts[..., :LAT] * f, axis=0)
        lat_s[pl.ds(4 * r, 4), :] = total / jnp.sum(li * f, axis=0)

    relay(0, 0)
    relay(1, 0)
    loads["k0"].wait()
    near0 = scores(0, 0)
    loads["k1"].wait()
    near1 = scores(1, 0)
    relay(0, 1)
    far0 = scores(0, 1)
    relay(1, 1)
    send_pair(0, *sums(0, near0, far0))
    far1 = scores(1, 1)
    send_rows(0)
    send_pair(1, *sums(1, near1, far1))
    send_rows(1)
    loads["vu"].wait()
    loads["w"].wait()
    finish_rows(0)
    finish_rows(1)

    latent = lat_s[...].astype(BF16)
    up0 = jnp.dot(latent, vu_s[0], preferred_element_type=F32)
    up1 = jnp.dot(latent, vu_s[1], preferred_element_type=F32)
    values = jnp.concatenate([up0, pltpu.roll(up1, 6, 0)], axis=1)
    row8 = lax.broadcasted_iota(jnp.int32, values.shape, 0)
    values = jnp.where(row8 < 2, values, pltpu.roll(values, 6, 0)).astype(BF16)

    def out_pair(g):
        return pltpu.make_async_remote_copy(
            src_ref=o_pair.at[g, 1 - c], dst_ref=o_pair_recv.at[g],
            send_sem=op_ss.at[g], recv_sem=op_rs.at[g],
            device_id=sibling, device_id_type=MESH)

    def o_copy(g, dz):
        return pltpu.make_async_remote_copy(
            src_ref=o_send.at[g, (z + dz) % NZ], dst_ref=o_recv.at[g, dz],
            send_sem=o_ss.at[g], recv_sem=o_rs.at[g],
            device_id=device(g, dz), device_id_type=MESH)

    def o_all(g):
        some = pl.ds(0, 8 if g else 7)
        return pltpu.make_async_remote_copy(
            src_ref=o_send.at[g, some], dst_ref=o_recv.at[g, some],
            send_sem=o_ss.at[g], recv_sem=o_rs.at[g],
            device_id=sibling, device_id_type=MESH)

    def project(g):
        cols = pl.ds(pl.multiple_of(((x + g) % NX) * XCOLS, XCOLS), XCOLS)
        share = jnp.dot(values, w_s[:, cols], preferred_element_type=F32)
        for j in range(NZ * NC):
            o_pair[g, j % NC, j // NC, :, pl.ds(0, DOUT)] = share[:4, j * DOUT:(j + 1) * DOUT]
        out_pair(g).start()

    def send_columns(g):
        out_pair(g).wait_recv()
        o_send[g] = (o_pair[g, c] + o_pair_recv[g]).astype(BF16)
        for dz in FAR_FIRST_Z:
            if g or dz:
                o_copy(g, dz).start()

    order = (2, 1, 3, 0)
    for g in order:
        project(g)
    for g in order:
        send_columns(g)
    o_recv[0, 0] = o_send[0, z]
    for g in range(NX):
        o_all(g).wait_recv()
    final = jnp.sum(o_recv[...].reshape(NCHIP, 4, 128).astype(F32), axis=0)
    for r in range(2):
        for q in range(2):
            at = 2 * r + q
            out_ref[r, pl.ds(q, 1), :] = final[at:at + 1, :DOUT]

    for r in range(2):
        for b in range(2):
            ag_all(r, b).wait_send()
            relay_copy(r, b).wait_send()
        pair_copy(r).wait_send()
        rs_all(r).wait_send()
    for g in range(NX):
        out_pair(g).wait_send()
        o_all(g).wait_send()


def per_device(queries, key_absorb, latent_cache, page_order, lengths, kerple_scale, kerple_rate,
               value_up, output_weight):
    any_spec = pl.BlockSpec(memory_space=pl.ANY)
    dma = pltpu.SemaphoreType.DMA
    out = pl.pallas_call(
        kernel,
        out_shape=jax.ShapeDtypeStruct((2, 2, DOUT), F32),
        in_specs=[any_spec] * 9,
        out_specs=pl.BlockSpec(memory_space=pltpu.VMEM),
        scratch_shapes=[
            pltpu.VMEM((2, 2, 2, NOPE + ROPE), BF16),
            pltpu.VMEM((8, NOPE + ROPE), F32),
            pltpu.VMEM((2, NOPE, LAT), BF16),
            pltpu.VMEM((2, WIDE, SLOTS), BF16),
            pltpu.SMEM((2, SLOTS // PAGE), jnp.int32),
            pltpu.SMEM((2,), jnp.int32),
            pltpu.VMEM((1, 128), F32),
            pltpu.VMEM((1, 128), F32),
            pltpu.VMEM((2, LAT, VDIM), BF16),
            pltpu.VMEM((2 * VDIM, D), BF16),
            pltpu.VMEM((2, NCHIP, 4, WIDE), BF16),
            pltpu.VMEM((64, WIDE), F32),
            pltpu.VMEM((2, 2, 2, 64, WIDE), BF16),
            pltpu.VMEM((2, ROWS, SLOTS), F32),
            pltpu.VMEM((ROWS, 128), F32),
            pltpu.VMEM((ROWS, 128), F32),
            pltpu.VMEM((2, HALF, WIDE), BF16),
            pltpu.VMEM((2, HALF, WIDE), BF16),
            pltpu.VMEM((HALF, WIDE), F32),
            pltpu.VMEM((2, NCHIP, 4, WIDE), BF16),
            pltpu.VMEM((2, NCHIP, 4, WIDE), BF16),
            pltpu.VMEM((8, LAT), F32),
            pltpu.VMEM((NX, NC, NZ, 4, 128), F32),
            pltpu.VMEM((NX, NZ, 4, 128), F32),
            pltpu.VMEM((NX, NZ, 4, 128), BF16),
            pltpu.VMEM((NX, NZ, 4, 128), BF16),
            dma((10,)),
            dma((2, 2)), dma((2, 2)),
            dma((2, 2)), dma((2, 2)),
            dma((2,)), dma((2,)),
            dma((2,)), dma((2,)),
            dma((NX,)), dma((NX,)),
            dma((NX,)), dma((NX,)),
        ],
        compiler_params=pltpu.CompilerParams(
            collective_id=0, has_side_effects=True, vmem_limit_bytes=56 * 1024 * 1024),
    )(
        queries, key_absorb, jnp.swapaxes(latent_cache, 1, 2), page_order, lengths,
        kerple_scale.reshape(1, 128), kerple_rate.reshape(1, 128), value_up, output_weight,
    )
    return out.astype(BF16)


def solution(mesh):
    in_specs = (
        P("rep", None, "ctx", None),
        P("ctx", None, None),
        P("rep", "ctx", None),
        P("rep", "ctx"),
        P("rep"),
        P(),
        P(),
        P("ctx", None, None),
        P("ctx", None),
    )
    out_specs = P("rep", None, "ctx")
    return jax.shard_map(
        per_device, mesh=mesh, in_specs=in_specs, out_specs=out_specs, check_vma=False
    )
```

time: 47.7 us -> 45.4 us (0.952)
  Pallas kernels: 46.4 us -> 44 us
    pallas_call x1, Pallas kernels: 46.4 us -> 44 us  [per_device(): pl.pallas_call(kernel, out_shape=jax.ShapeDtypeStruct((2, 2, DOUT), F32),...]
where the time goes in v3:
time: 45.4 us; the launch traced here: 45.3 us
  Pallas kernels  44 us (97%)
  other arithmetic  1.25 us (3%)
    pallas_call x1, Pallas kernels, per_device(): pl.pallas_call(kernel, out_shape=jax.ShapeDtypeStruct((2, 2, DOUT), F32),...  44 us
    convert_element_type x1, other arithmetic, per_device(): return out.astype(BF16)  1.25 us

profile of v3, /device:TPU:1, one launch (start us, length us, event | category | flops | bytes accessed | tf_op | source)
XLA Modules:
  0.0 45.3 jit_solution(7169570173062477847)
XLA Ops:
  0.0 44.0 %shard_map.91 = f32[2,2,112]{2,1,0:T(2,128)} custom-call(bf16[2,2,2,192]{3,2,1,0:T(2,128)(2,1)} %q_hbm.1, bf16[2,128,512]{2,1,0:T(8,128)(2,1)} %ka_hbm.1, bf16[2,576,4096]{2,1,0:T(8,128)(2,1)} %bitcast.3, s32[2,32]{1,0:T(2,128)} %page_hbm.1, s32[2]{0:T(128)} %len_hbm.1, f32[1,128]{1,0:T(1,128)} %bitcast.4, f32[1,128]{1,0:T(1,128)} %bitcast.5, ...), custom_call_target="tpu_custom_call" | custom-call | tf_op jit(solution)/shard_map/pallas_call | solution.py:369
  44.0 1.2 %convert_element_type.3 = bf16[2,2,112]{2,1,0:T(2,128)(2,1)} convert(f32[2,2,112]{2,1,0:T(2,128)} %shard_map.91) | non-fusion elementwise | flops 448 | bytes 2688 | tf_op jit(solution)/shard_map/convert_element_type | solution.py:415

commit v4 on v3

--- a/solution.py
+++ b/solution.py
@@ -69,9 +69,9 @@
     out_ref,
     q_s, x_s, ka_s, kt_s, page_s, len_s, scale_s, rate_s, vu_s, w_s,
     qin, qf, qall, s_buf, rate_b, scale_b,
-    pair_send, pair_recv, rs_f, rs_send, rs_recv, lat_s, o_pair, o_pair_recv, o_send, o_recv,
+    v_s, pair_send, pair_recv, rs_send, rs_recv, lat_s, o_send, o_recv,
     local_sem, ag_ss, ag_rs, relay_ss, relay_rs, pair_ss, pair_rs, rs_ss, rs_rs,
-    op_ss, op_rs, o_ss, o_rs,
+    o_ss, o_rs,
 ):
     ctx = lax.axis_index("ctx")
     rep = lax.axis_index("rep")
@@ -144,15 +144,15 @@
             src_ref=some, dst_ref=some, send_sem=ag_ss.at[r, b], recv_sem=ag_rs.at[r, b],
             device_id=sibling, device_id_type=MESH)
 
-    for b in range(2):
-        for r in range(2):
+    for r in range(2):
+        for b in range(2):
             for t in AWAY:
                 if t // 16 == b:
                     ag_copy(r, t).start()
 
     for r in range(2):
         kt_s[r, pl.ds(LAT + ROPE, 64), :] = jnp.zeros((64, SLOTS), BF16)
-    o_pair[...] = jnp.zeros_like(o_pair)
+    o_send[...] = jnp.zeros_like(o_send)
     row = lax.broadcasted_iota(jnp.int32, (ROWS, 128), 0)
     lane = lax.broadcasted_iota(jnp.int32, (ROWS, 128), 1)
     slot = (row // 128) * 16 + (row // 4) % 16
@@ -169,6 +169,11 @@
     scale_b[...] = jnp.broadcast_to(scale_col * (1.0 / SIGMA), (ROWS, 128))
     loads["page"].wait()
     loads["len"].wait()
+    for r in range(2):
+        loads["k%d" % r].wait()
+        for i in range(8):
+            cols = pl.ds(i * (SLOTS // 8), SLOTS // 8)
+            v_s[r, cols, :] = kt_s[r, pl.ds(0, LAT), cols].T
 
     def relay_copy(r, b):
         return pltpu.make_async_remote_copy(
@@ -205,73 +210,69 @@
             peak = jnp.maximum(peak, u)
         return jnp.max(peak, axis=-1, keepdims=True)
 
-    def sums(r, near, far):
-        shift = jnp.concatenate([near, far], axis=0)
-        total = jnp.zeros((32, 8, 128), F32)
+    def sums(r, b, shift):
+        total = jnp.zeros((16, 8, 128), F32)
         weights = []
         for p in range(SLOTS // PAGE):
-            u = s_buf[r, :, pl.ds(p * PAGE, PAGE)].reshape(32, 8, 128)
+            u = s_buf[r, pl.ds(HALF * b, HALF), pl.ds(p * PAGE, PAGE)].reshape(16, 8, 128)
             w = jnp.exp2(KAPPA * (u - shift))
             total = total + w
-            weights.append(w.reshape(ROWS, 128).astype(BF16))
-        summed = lax.dot_general(
-            jnp.concatenate(weights, axis=1), kt_s[r, pl.ds(0, LAT), :],
-            (((1,), (1,)), ((), ())), preferred_element_type=F32)
-        return shift, jnp.sum(total, axis=-1, keepdims=True), summed
-
-    def pair_copy(r):
-        return pltpu.make_async_remote_copy(
-            src_ref=pair_send.at[r], dst_ref=pair_recv.at[r],
-            send_sem=pair_ss.at[r], recv_sem=pair_rs.at[r],
-            device_id=sibling, device_id_type=MESH)
-
-    def send_pair(r, shift, total, summed):
-        stats = pack_stats(
-            jnp.broadcast_to(shift, (32, 8, 128)), jnp.broadcast_to(total, (32, 8, 128)))
-        stats = stats.reshape(2, 2, 64, 128)
-        summed = summed.reshape(2, 2, 64, LAT)
-        for b in range(2):
-            rows = pl.ds(64 * b, 64)
-            pair_send[r, rows, pl.ds(0, LAT)] = summed[b, 1].astype(BF16)
-            pair_send[r, rows, pl.ds(LAT, 128)] = stats[b, 1].astype(BF16)
-        pair_copy(r).start()
-        for b in range(2):
-            rows = pl.ds(64 * b, 64)
-            rs_f[rows, pl.ds(0, LAT)] = summed[b, 0]
-            rs_f[rows, pl.ds(LAT, 128)] = stats[b, 0]
+            weights.append(w.reshape(HALF, 128).astype(BF16))
+        summed = jnp.dot(jnp.concatenate(weights, axis=1), v_s[r], preferred_element_type=F32)
+        return jnp.sum(total, axis=-1, keepdims=True), summed
+
+    def pair_copy(r, b):
+        return pltpu.make_async_remote_copy(
+            src_ref=pair_send.at[r, b], dst_ref=pair_recv.at[r, b],
+            send_sem=pair_ss.at[r, b], recv_sem=pair_rs.at[r, b],
+            device_id=sibling, device_id_type=MESH)
+
+    def attend(r, b, shift):
+        total, summed = sums(r, b, shift)
+        shift = jnp.broadcast_to(shift, (16, 8, 128))
+        total = jnp.broadcast_to(total, (16, 8, 128))
+        pair_send[r, b, :, pl.ds(0, LAT)] = summed[64:].astype(BF16)
+        pair_send[r, b, :, pl.ds(LAT, 128)] = pack_stats(shift[8:], total[8:]).reshape(64, 128).astype(BF16)
+        pair_copy(r, b).start()
+        return shift[:8, :, :1], total[:8, :, :1], summed[:64].reshape(8, 8, LAT)
 
     def rs_copy(r, t):
         return pltpu.make_async_remote_copy(
             src_ref=rs_send.at[r, t], dst_ref=rs_recv.at[r, t],
-            send_sem=rs_ss.at[r], recv_sem=rs_rs.at[r],
+            send_sem=rs_ss.at[r, t // 16], recv_sem=rs_rs.at[r, t // 16],
             device_id=back(t), device_id_type=MESH)
 
-    def rs_all(r):
-        return pltpu.make_async_remote_copy(
-            src_ref=rs_send.at[r, pl.ds(0, NCHIP - 1)], dst_ref=rs_recv.at[r, pl.ds(0, NCHIP - 1)],
-            send_sem=rs_ss.at[r], recv_sem=rs_rs.at[r],
-            device_id=sibling, device_id_type=MESH)
-
-    def send_rows(r):
-        pair_copy(r).wait_recv()
-        mine = rs_f[...].reshape(16, 8, WIDE)
-        theirs = pair_recv[r].astype(F32).reshape(16, 8, WIDE)
-        (c0, l0), (c1, l1) = unpack_stats(mine[..., LAT:]), unpack_stats(theirs[..., LAT:])
+    def rs_all(r, b):
+        some = pl.ds(0, 15 if b == 0 else 16)
+        return pltpu.make_async_remote_copy(
+            src_ref=rs_send.at[r, some], dst_ref=rs_recv.at[r, some],
+            send_sem=rs_ss.at[r, b], recv_sem=rs_rs.at[r, b],
+            device_id=sibling, device_id_type=MESH)
+
+    def send_rows(r, b, own):
+        c0, l0, mine = own
+        pair_copy(r, b).wait_recv()
+        theirs = pair_recv[r, b].astype(F32).reshape(8, 8, WIDE)
+        c1, l1 = unpack_stats(theirs[..., LAT:])
         shift = jnp.maximum(c0, c1)
         f0, f1 = jnp.exp2(KAPPA * (c0 - shift)), jnp.exp2(KAPPA * (c1 - shift))
-        both = mine[..., :LAT] * f0 + theirs[..., :LAT] * f1
+        both = mine * f0 + theirs[..., :LAT] * f1
         stats = pack_stats(
-            jnp.broadcast_to(shift, (16, 8, 128)), jnp.broadcast_to(l0 * f0 + l1 * f1, (16, 8, 128)))
-        for i in range(NCHIP // 2):
+            jnp.broadcast_to(shift, (8, 8, 128)), jnp.broadcast_to(l0 * f0 + l1 * f1, (8, 8, 128)))
+        for i in range(8):
             for h in range(2):
-                rs_send[r, 2 * i + h, :, pl.ds(0, LAT)] = both[i, 4 * h:4 * h + 4].astype(BF16)
-                rs_send[r, 2 * i + h, :, pl.ds(LAT, 128)] = stats[i, 4 * h:4 * h + 4].astype(BF16)
+                t = 16 * b + 2 * i + h
+                rs_send[r, t, :, pl.ds(0, LAT)] = both[i, 4 * h:4 * h + 4].astype(BF16)
+                rs_send[r, t, :, pl.ds(LAT, 128)] = stats[i, 4 * h:4 * h + 4].astype(BF16)
         for t in AWAY:
-            rs_copy(r, t).start()
-        rs_recv[r, SELF] = rs_send[r, SELF]
+            if t // 16 == b:
+                rs_copy(r, t).start()
+        if b == 0:
+            rs_recv[r, SELF] = rs_send[r, SELF]
 
     def finish_rows(r):
-        rs_all(r).wait_recv()
+        rs_all(r, 0).wait_recv()
+        rs_all(r, 1).wait_recv()
         parts = rs_recv[r].astype(F32)
         ci, li = unpack_stats(parts[..., LAT:])
         f = jnp.exp2(KAPPA * (ci - jnp.max(ci, axis=0, keepdims=True)))
@@ -279,19 +280,21 @@
         lat_s[pl.ds(4 * r, 4), :] = total / jnp.sum(li * f, axis=0)
 
     relay(0, 0)
-    relay(1, 0)
-    loads["k0"].wait()
     near0 = scores(0, 0)
-    loads["k1"].wait()
-    near1 = scores(1, 0)
     relay(0, 1)
     far0 = scores(0, 1)
+    relay(1, 0)
+    far0 = attend(0, 1, far0)
+    near0 = attend(0, 0, near0)
+    send_rows(0, 1, far0)
+    near1 = scores(1, 0)
     relay(1, 1)
-    send_pair(0, *sums(0, near0, far0))
+    send_rows(0, 0, near0)
     far1 = scores(1, 1)
-    send_rows(0)
-    send_pair(1, *sums(1, near1, far1))
-    send_rows(1)
+    far1 = attend(1, 1, far1)
+    near1 = attend(1, 0, near1)
+    send_rows(1, 1, far1)
+    send_rows(1, 0, near1)
     loads["vu"].wait()
     loads["w"].wait()
     finish_rows(0)
@@ -304,17 +307,12 @@
     row8 = lax.broadcasted_iota(jnp.int32, values.shape, 0)
     values = jnp.where(row8 < 2, values, pltpu.roll(values, 6, 0)).astype(BF16)
 
-    def out_pair(g):
-        return pltpu.make_async_remote_copy(
-            src_ref=o_pair.at[g, 1 - c], dst_ref=o_pair_recv.at[g],
-            send_sem=op_ss.at[g], recv_sem=op_rs.at[g],
-            device_id=sibling, device_id_type=MESH)
-
-    def o_copy(g, dz):
-        return pltpu.make_async_remote_copy(
-            src_ref=o_send.at[g, (z + dz) % NZ], dst_ref=o_recv.at[g, dz],
+    def o_copy(g, dz, dc):
+        zz, cc = (z + dz) % NZ, (c + dc) % NC
+        return pltpu.make_async_remote_copy(
+            src_ref=o_send.at[g, zz, cc], dst_ref=o_recv.at[g, dz, dc],
             send_sem=o_ss.at[g], recv_sem=o_rs.at[g],
-            device_id=device(g, dz), device_id_type=MESH)
+            device_id=((((x + g) % NX) * NZ + zz) * NC + cc, rep), device_id_type=MESH)
 
     def o_all(g):
         some = pl.ds(0, 8 if g else 7)
@@ -323,29 +321,27 @@
             send_sem=o_ss.at[g], recv_sem=o_rs.at[g],
             device_id=sibling, device_id_type=MESH)
 
-    def project(g):
+    def sib_copy():
+        return pltpu.make_async_remote_copy(
+            src_ref=o_send.at[0, z, 1 - c], dst_ref=o_recv.at[0, 0, 1],
+            send_sem=o_ss.at[NX], recv_sem=o_rs.at[NX],
+            device_id=sibling, device_id_type=MESH)
+
+    for g in (2, 1, 3, 0):
         cols = pl.ds(pl.multiple_of(((x + g) % NX) * XCOLS, XCOLS), XCOLS)
         share = jnp.dot(values, w_s[:, cols], preferred_element_type=F32)
         for j in range(NZ * NC):
-            o_pair[g, j % NC, j // NC, :, pl.ds(0, DOUT)] = share[:4, j * DOUT:(j + 1) * DOUT]
-        out_pair(g).start()
-
-    def send_columns(g):
-        out_pair(g).wait_recv()
-        o_send[g] = (o_pair[g, c] + o_pair_recv[g]).astype(BF16)
+            o_send[g, j // NC, j % NC, :, pl.ds(0, DOUT)] = share[:4, j * DOUT:(j + 1) * DOUT].astype(BF16)
         for dz in FAR_FIRST_Z:
             if g or dz:
-                o_copy(g, dz).start()
-
-    order = (2, 1, 3, 0)
-    for g in order:
-        project(g)
-    for g in order:
-        send_columns(g)
-    o_recv[0, 0] = o_send[0, z]
-    for g in range(NX):
+                for dc in range(NC):
+                    o_copy(g, dz, dc).start()
+    sib_copy().start()
+    o_recv[0, 0, 0] = o_send[0, z, c]
+    for g in (0, 1, 3, 2):
         o_all(g).wait_recv()
-    final = jnp.sum(o_recv[...].reshape(NCHIP, 4, 128).astype(F32), axis=0)
+    sib_copy().wait_recv()
+    final = jnp.sum(o_recv[...].reshape(NCHIP * NC, 4, 128).astype(F32), axis=0)
     for r in range(2):
         for q in range(2):
             at = 2 * r + q
@@ -355,11 +351,11 @@
         for b in range(2):
             ag_all(r, b).wait_send()
             relay_copy(r, b).wait_send()
-        pair_copy(r).wait_send()
-        rs_all(r).wait_send()
+            pair_copy(r, b).wait_send()
+            rs_all(r, b).wait_send()
     for g in range(NX):
-        out_pair(g).wait_send()
         o_all(g).wait_send()
+    sib_copy().wait_send()
 
 
 def per_device(queries, key_absorb, latent_cache, page_order, lengths, kerple_scale, kerple_rate,
@@ -388,23 +384,20 @@
             pltpu.VMEM((2, ROWS, SLOTS), F32),
             pltpu.VMEM((ROWS, 128), F32),
             pltpu.VMEM((ROWS, 128), F32),
-            pltpu.VMEM((2, HALF, WIDE), BF16),
-            pltpu.VMEM((2, HALF, WIDE), BF16),
-            pltpu.VMEM((HALF, WIDE), F32),
+            pltpu.VMEM((2, SLOTS, LAT), BF16),
+            pltpu.VMEM((2, 2, 64, WIDE), BF16),
+            pltpu.VMEM((2, 2, 64, WIDE), BF16),
             pltpu.VMEM((2, NCHIP, 4, WIDE), BF16),
             pltpu.VMEM((2, NCHIP, 4, WIDE), BF16),
             pltpu.VMEM((8, LAT), F32),
-            pltpu.VMEM((NX, NC, NZ, 4, 128), F32),
-            pltpu.VMEM((NX, NZ, 4, 128), F32),
-            pltpu.VMEM((NX, NZ, 4, 128), BF16),
-            pltpu.VMEM((NX, NZ, 4, 128), BF16),
+            pltpu.VMEM((NX, NZ, NC, 4, 128), BF16),
+            pltpu.VMEM((NX, NZ, NC, 4, 128), BF16),
             dma((10,)),
             dma((2, 2)), dma((2, 2)),
             dma((2, 2)), dma((2, 2)),
-            dma((2,)), dma((2,)),
-            dma((2,)), dma((2,)),
-            dma((NX,)), dma((NX,)),
-            dma((NX,)), dma((NX,)),
+            dma((2, 2)), dma((2, 2)),
+            dma((2, 2)), dma((2, 2)),
+            dma((NX + 1,)), dma((NX + 1,)),
         ],
         compiler_params=pltpu.CompilerParams(
             collective_id=0, has_side_effects=True, vmem_limit_bytes=56 * 1024 * 1024),

time: 45.4 us -> 45 us (level)
  no operation moved by 1% of the time
where the time goes in v4:
time: 45 us; the launch traced here: 44.9 us
  Pallas kernels  43.6 us (97%)
  other arithmetic  1.25 us (3%)
    pallas_call x1, Pallas kernels, per_device(): pl.pallas_call(kernel, out_shape=jax.ShapeDtypeStruct((2, 2, DOUT), F32),...  43.6 us
    convert_element_type x1, other arithmetic, per_device(): return out.astype(BF16)  1.25 us

profile of v4, /device:TPU:1, one launch (start us, length us, event | category | flops | bytes accessed | tf_op | source)
XLA Modules:
  0.0 44.9 jit_solution(10012005777771755746)
XLA Ops:
  0.0 43.6 %shard_map.91 = f32[2,2,112]{2,1,0:T(2,128)} custom-call(bf16[2,2,2,192]{3,2,1,0:T(2,128)(2,1)} %q_hbm.1, bf16[2,128,512]{2,1,0:T(8,128)(2,1)} %ka_hbm.1, bf16[2,576,4096]{2,1,0:T(8,128)(2,1)} %bitcast.3, s32[2,32]{1,0:T(2,128)} %page_hbm.1, s32[2]{0:T(128)} %len_hbm.1, f32[1,128]{1,0:T(1,128)} %bitcast.4, f32[1,128]{1,0:T(1,128)} %bitcast.5, ...), custom_call_target="tpu_custom_call" | custom-call | tf_op jit(solution)/shard_map/pallas_call | solution.py:365
  43.6 1.2 %convert_element_type.3 = bf16[2,2,112]{2,1,0:T(2,128)(2,1)} convert(f32[2,2,112]{2,1,0:T(2,128)} %shard_map.91) | non-fusion elementwise | flops 448 | bytes 2688 | tf_op jit(solution)/shard_map/convert_element_type | solution.py:408

commit v5 on v4

--- a/solution.py
+++ b/solution.py
@@ -68,7 +68,7 @@
     q_hbm, ka_hbm, kt_hbm, page_hbm, len_hbm, scale_hbm, rate_hbm, vu_hbm, w_hbm,
     out_ref,
     q_s, x_s, ka_s, kt_s, page_s, len_s, scale_s, rate_s, vu_s, w_s,
-    qin, qf, qall, s_buf, rate_b, scale_b,
+    qin0, qin1, qf, qall, s_buf, rate_b, scale_b,
     v_s, pair_send, pair_recv, rs_send, rs_recv, lat_s, o_send, o_recv,
     local_sem, ag_ss, ag_rs, relay_ss, relay_rs, pair_ss, pair_rs, rs_ss, rs_rs,
     o_ss, o_rs,
@@ -105,13 +105,15 @@
             ("page", page_hbm, page_s),
             ("len", len_hbm, len_s),
             ("k0", kt_hbm.at[0], kt_s.at[0, pl.ds(0, LAT + ROPE)]),
-            ("k1", kt_hbm.at[1], kt_s.at[1, pl.ds(0, LAT + ROPE)]),
+            ("k1", kt_hbm.at[1, pl.ds(0, LAT)], kt_s.at[1, pl.ds(0, LAT)]),
+            ("k1r", kt_hbm.at[1, pl.ds(LAT, ROPE)], kt_s.at[1, pl.ds(LAT + ROPE, ROPE)]),
             ("vu", vu_hbm, vu_s),
             ("w", w_hbm, w_s),
         ))
     }
-    for load in loads.values():
-        load.start()
+    for name, load in loads.items():
+        if name not in ("vu", "w"):
+            load.start()
 
     loads["q"].wait()
     for r in range(2):
@@ -125,33 +127,13 @@
     lat1 = jnp.dot(nope, ka_s[1], preferred_element_type=F32)
     row8 = lax.broadcasted_iota(jnp.int32, (8, LAT), 0)
     lat = jnp.where((row8 // 2) % 2 == 0, lat0, lat1)
-    for r in range(2):
-        qin[r, SELF, :, pl.ds(0, LAT)] = lat[4 * r:4 * r + 4].astype(BF16)
-        qin[r, SELF, :, pl.ds(LAT, 128)] = jnp.zeros((4, 128), BF16)
-        qin[r, SELF, :, pl.ds(LAT, ROPE)] = xq[4 * r:4 * r + 4, NOPE:].astype(BF16)
-
-    pl.semaphore_wait(barrier, len(AWAY) + 1)
-
-    def ag_copy(r, t):
-        return pltpu.make_async_remote_copy(
-            src_ref=qin.at[r, SELF], dst_ref=qin.at[r, t],
-            send_sem=ag_ss.at[r, t // 16], recv_sem=ag_rs.at[r, t // 16],
-            device_id=toward(t), device_id_type=MESH)
-
-    def ag_all(r, b):
-        some = qin.at[r, pl.ds(0, 15 if b == 0 else 16)]
-        return pltpu.make_async_remote_copy(
-            src_ref=some, dst_ref=some, send_sem=ag_ss.at[r, b], recv_sem=ag_rs.at[r, b],
-            device_id=sibling, device_id_type=MESH)
-
-    for r in range(2):
-        for b in range(2):
-            for t in AWAY:
-                if t // 16 == b:
-                    ag_copy(r, t).start()
-
-    for r in range(2):
-        kt_s[r, pl.ds(LAT + ROPE, 64), :] = jnp.zeros((64, SLOTS), BF16)
+    qin0[SELF, :, pl.ds(0, LAT)] = lat[:4].astype(BF16)
+    qin0[SELF, :, pl.ds(LAT, ROPE)] = xq[:4, NOPE:].astype(BF16)
+    qin0[SELF, :, pl.ds(LAT + ROPE, ROPE)] = xq[4:, NOPE:].astype(BF16)
+    qin1[SELF] = lat[4:].astype(BF16)
+
+    kt_s[0, pl.ds(LAT + ROPE, ROPE), :] = jnp.zeros((ROPE, SLOTS), BF16)
+    kt_s[1, pl.ds(LAT, ROPE), :] = jnp.zeros((ROPE, SLOTS), BF16)
     o_send[...] = jnp.zeros_like(o_send)
     row = lax.broadcasted_iota(jnp.int32, (ROWS, 128), 0)
     lane = lax.broadcasted_iota(jnp.int32, (ROWS, 128), 1)
@@ -169,12 +151,42 @@
     scale_b[...] = jnp.broadcast_to(scale_col * (1.0 / SIGMA), (ROWS, 128))
     loads["page"].wait()
     loads["len"].wait()
-    for r in range(2):
-        loads["k%d" % r].wait()
+
+    def transpose(r):
         for i in range(8):
             cols = pl.ds(i * (SLOTS // 8), SLOTS // 8)
             v_s[r, cols, :] = kt_s[r, pl.ds(0, LAT), cols].T
 
+    pl.semaphore_wait(barrier, len(AWAY) + 1)
+
+    qin = (qin0, qin1)
+
+    def ag_copy(r, t):
+        return pltpu.make_async_remote_copy(
+            src_ref=qin[r].at[SELF], dst_ref=qin[r].at[t],
+            send_sem=ag_ss.at[r, t // 16], recv_sem=ag_rs.at[r, t // 16],
+            device_id=toward(t), device_id_type=MESH)
+
+    def ag_all(r, b):
+        some = qin[r].at[pl.ds(0, 15 if b == 0 else 16)]
+        return pltpu.make_async_remote_copy(
+            src_ref=some, dst_ref=some, send_sem=ag_ss.at[r, b], recv_sem=ag_rs.at[r, b],
+            device_id=sibling, device_id_type=MESH)
+
+    for r, b in ((0, 0), (0, 1), (1, 1), (1, 0)):
+        for t in AWAY:
+            if t // 16 == b:
+                ag_copy(r, t).start()
+
+
+    loads["k0"].wait()
+    transpose(0)
+    loads["k1"].wait()
+    loads["k1r"].wait()
+    loads["vu"].start()
+    loads["w"].start()
+    transpose(1)
+
     def relay_copy(r, b):
         return pltpu.make_async_remote_copy(
             src_ref=qall.at[r, b, 0], dst_ref=qall.at[r, b, 1],
@@ -183,9 +195,13 @@
 
     def relay(r, b):
         ag_all(r, b).wait_recv()
-        for i in range(8):
-            qf[pl.ds(8 * i, 4), :] = qin[r, 16 * b + 2 * i].astype(F32)
-            qf[pl.ds(8 * i + 4, 4), :] = qin[r, 16 * b + 2 * i + 1].astype(F32)
+        for i in range(16):
+            t, rows = 16 * b + i, pl.ds(4 * i, 4)
+            if r == 0:
+                qf[rows, :] = qin0[t].astype(F32)
+            else:
+                qf[rows, pl.ds(0, LAT)] = qin1[t].astype(F32)
+                qf[rows, pl.ds(LAT, 128)] = qin0[t, :, pl.ds(LAT, 128)].astype(F32)
         qall[r, b, 0] = qf[...].astype(BF16)
         relay_copy(r, b).start()
 
@@ -282,18 +298,18 @@
     relay(0, 0)
     near0 = scores(0, 0)
     relay(0, 1)
+    near0 = attend(0, 0, near0)
     far0 = scores(0, 1)
-    relay(1, 0)
+    relay(1, 1)
     far0 = attend(0, 1, far0)
-    near0 = attend(0, 0, near0)
-    send_rows(0, 1, far0)
-    near1 = scores(1, 0)
-    relay(1, 1)
     send_rows(0, 0, near0)
     far1 = scores(1, 1)
+    relay(1, 0)
+    send_rows(0, 1, far0)
     far1 = attend(1, 1, far1)
+    near1 = scores(1, 0)
+    send_rows(1, 1, far1)
     near1 = attend(1, 0, near1)
-    send_rows(1, 1, far1)
     send_rows(1, 0, near1)
     loads["vu"].wait()
     loads["w"].wait()
@@ -378,7 +394,8 @@
             pltpu.VMEM((1, 128), F32),
             pltpu.VMEM((2, LAT, VDIM), BF16),
             pltpu.VMEM((2 * VDIM, D), BF16),
-            pltpu.VMEM((2, NCHIP, 4, WIDE), BF16),
+            pltpu.VMEM((NCHIP, 4, WIDE), BF16),
+            pltpu.VMEM((NCHIP, 4, LAT), BF16),
             pltpu.VMEM((64, WIDE), F32),
             pltpu.VMEM((2, 2, 2, 64, WIDE), BF16),
             pltpu.VMEM((2, ROWS, SLOTS), F32),
@@ -392,7 +409,7 @@
             pltpu.VMEM((8, LAT), F32),
             pltpu.VMEM((NX, NZ, NC, 4, 128), BF16),
             pltpu.VMEM((NX, NZ, NC, 4, 128), BF16),
-            dma((10,)),
+            dma((11,)),
             dma((2, 2)), dma((2, 2)),
             dma((2, 2)), dma((2, 2)),
             dma((2, 2)), dma((2, 2)),

time: 45 us -> 43.9 us (0.976)
  Pallas kernels: 43.6 us -> 42.5 us
    pallas_call x1, Pallas kernels: 43.6 us -> 42.5 us  [per_device(): pl.pallas_call(kernel, out_shape=jax.ShapeDtypeStruct((2, 2, DOUT), F32),...]
where the time goes in v5:
time: 43.9 us; the launch traced here: 43.8 us
  Pallas kernels  42.5 us (97%)
  other arithmetic  1.25 us (3%)
    pallas_call x1, Pallas kernels, per_device(): pl.pallas_call(kernel, out_shape=jax.ShapeDtypeStruct((2, 2, DOUT), F32),...  42.5 us
    convert_element_type x1, other arithmetic, per_device(): return out.astype(BF16)  1.25 us

profile of v5, /device:TPU:1, one launch (start us, length us, event | category | flops | bytes accessed | tf_op | source)
XLA Modules:
  0.0 43.8 jit_solution(16353951681097789700)
XLA Ops:
  0.0 42.5 %shard_map.91 = f32[2,2,112]{2,1,0:T(2,128)} custom-call(bf16[2,2,2,192]{3,2,1,0:T(2,128)(2,1)} %q_hbm.1, bf16[2,128,512]{2,1,0:T(8,128)(2,1)} %ka_hbm.1, bf16[2,576,4096]{2,1,0:T(8,128)(2,1)} %bitcast.3, s32[2,32]{1,0:T(2,128)} %page_hbm.1, s32[2]{0:T(128)} %len_hbm.1, f32[1,128]{1,0:T(1,128)} %bitcast.4, f32[1,128]{1,0:T(1,128)} %bitcast.5, ...), custom_call_target="tpu_custom_call" | custom-call | tf_op jit(solution)/shard_map/pallas_call | solution.py:381
  42.5 1.2 %convert_element_type.3 = bf16[2,2,112]{2,1,0:T(2,128)(2,1)} convert(f32[2,2,112]{2,1,0:T(2,128)} %shard_map.91) | non-fusion elementwise | flops 448 | bytes 2688 | tf_op jit(solution)/shard_map/convert_element_type | solution.py:425

commit v6 on v5

--- a/solution.py
+++ b/solution.py
@@ -304,8 +304,8 @@
     far0 = attend(0, 1, far0)
     send_rows(0, 0, near0)
     far1 = scores(1, 1)
+    send_rows(0, 1, far0)
     relay(1, 0)
-    send_rows(0, 1, far0)
     far1 = attend(1, 1, far1)
     near1 = scores(1, 0)
     send_rows(1, 1, far1)

time: 43.9 us -> 43.7 us (level)
  no operation moved by 1% of the time
where the time goes in v6:
time: 43.7 us; the launch traced here: 43.6 us
  Pallas kernels  42.3 us (97%)
  other arithmetic  1.25 us (3%)
    pallas_call x1, Pallas kernels, per_device(): pl.pallas_call(kernel, out_shape=jax.ShapeDtypeStruct((2, 2, DOUT), F32),...  42.3 us
    convert_element_type x1, other arithmetic, per_device(): return out.astype(BF16)  1.25 us

profile of v6, /device:TPU:1, one launch (start us, length us, event | category | flops | bytes accessed | tf_op | source)
XLA Modules:
  0.0 43.6 jit_solution(11975333163079454108)
XLA Ops:
  0.0 42.3 %shard_map.91 = f32[2,2,112]{2,1,0:T(2,128)} custom-call(bf16[2,2,2,192]{3,2,1,0:T(2,128)(2,1)} %q_hbm.1, bf16[2,128,512]{2,1,0:T(8,128)(2,1)} %ka_hbm.1, bf16[2,576,4096]{2,1,0:T(8,128)(2,1)} %bitcast.3, s32[2,32]{1,0:T(2,128)} %page_hbm.1, s32[2]{0:T(128)} %len_hbm.1, f32[1,128]{1,0:T(1,128)} %bitcast.4, f32[1,128]{1,0:T(1,128)} %bitcast.5, ...), custom_call_target="tpu_custom_call" | custom-call | tf_op jit(solution)/shard_map/pallas_call | solution.py:381
  42.3 1.2 %convert_element_type.3 = bf16[2,2,112]{2,1,0:T(2,128)(2,1)} convert(f32[2,2,112]{2,1,0:T(2,128)} %shard_map.91) | non-fusion elementwise | flops 448 | bytes 2688 | tf_op jit(solution)/shard_map/convert_element_type | solution.py:425
